TPU v7x, 512 devices: a whole 4x8x8 slice. The times are simulated.
512 devices in a mesh: space: 64 (over z, y_hi, x), summ: 8 (over y_lo, core).
Axes of the slice: x: 4, y: 8 (y_hi: 2, y_lo: 4; y = y_hi * 4 + y_lo), z: 8, core: 2. Of those that a mesh axis runs over, the one named last changes fastest.
Arguments:
- tokens: bfloat16 [64, 8, 32, 1024], P('space', None, None, 'summ'), may hold values from -8 to 8
- tile_map: int32 [64], replicated, may hold values from 0 to 63, each once
- norm_gain: float32 [1024], replicated, may hold values from 0.5 to 1.5
- q_weight: bfloat16 [1024, 1024], P(None, 'summ'), may hold values from -1.5 to 1.5
- k_weight: bfloat16 [1024, 1024], P(None, 'summ'), may hold values from -1.5 to 1.5
- v_weight: bfloat16 [1024, 1024], P(None, 'summ'), may hold values from -0.1875 to 0.1875
- out_weight: bfloat16 [1024, 1024], P('summ'), may hold values from -0.1875 to 0.1875
- pos_bias: float32 [16, 7, 7], P('summ'), may hold values from 1 to 4
- sum_keys: bfloat16 [4096, 1024], P('summ'), may hold values from -64 to 64
- sum_values: bfloat16 [4096, 1024], P('summ'), may hold values from -6 to 6
Outputs:
- mixed: bfloat16 [64, 8, 32, 1024], P('space', None, None, 'summ')
Inputs may be any that keep to these rules, and one draw needn't show every extreme that they name: Block b of tokens holds the grid tile tile_map[b], counted row by row with 8 tiles a row; every tile is held once.
All inputs are finite; a program needn't handle non-finite values.
Results may differ from a plain program's by a relative error of at most 0.02.
Values may be sent and summed in bfloat16 or wider, within the bound.
A program may use at most 128 MiB of HBM per device.

v0:
```python
from functools import partial

import jax
import jax.numpy as jnp
from jax import lax
from jax.sharding import PartitionSpec as P

D = 1024
HD = 64
HALO = 3
TX = 8
BW = 32
BH = 8


EPSILON = 1e-05


def combined_all(value, axis, join):
    pieces = jax.tree.map(lambda part: lax.all_gather(part, axis), value)
    head = jax.tree.map(lambda part: part[0], pieces)
    tail = jax.tree.map(lambda part: part[1:], pieces)
    so_far, _ = lax.scan(lambda so_far, slab: (join(so_far, slab), None), head, tail)
    return so_far


def normalize(raw_values, norm_gain):
    floats = raw_values.astype(jnp.float32)
    mean_square = jnp.mean(floats * floats, axis=-1, keepdims=True)
    return (floats * lax.rsqrt(mean_square + EPSILON) * norm_gain).astype(jnp.bfloat16)


def summary_part(query_rows, key_rows, value_rows):
    scores = jnp.dot(query_rows, key_rows.T, preferred_element_type=jnp.float32) * HD ** (-0.5)
    row_max = jnp.max(scores, axis=-1)
    weights = jnp.exp(scores - row_max[:, None])
    weight_sum = jnp.sum(weights, axis=-1)
    weighted = jnp.dot(weights.astype(jnp.bfloat16), value_rows, preferred_element_type=jnp.float32)
    return (row_max, weight_sum, weighted)


def summary_heads(query_rows, key_rows, value_rows, head_count):
    token_count = query_rows.shape[0]
    summary_rows = key_rows.shape[0]
    query_heads = query_rows.reshape(token_count, head_count, HD).transpose(1, 0, 2)
    key_heads = key_rows.reshape(summary_rows, head_count, HD).transpose(1, 0, 2)
    value_heads = value_rows.reshape(summary_rows, head_count, HD).transpose(1, 0, 2)

    def one_head(operands):
        return summary_part(operands[0], operands[1], operands[2])

    maxima, sums, weighted = lax.map(one_head, (query_heads, key_heads, value_heads))
    return (maxima.T, sums.T, weighted.transpose(1, 0, 2).reshape(token_count, head_count * HD))


def merge_parts(left_part, right_part):
    joint_max = jnp.maximum(left_part[0], right_part[0])
    left_factor = jnp.exp(left_part[0] - joint_max)
    right_factor = jnp.exp(right_part[0] - joint_max)
    weight_sum = left_part[1] * left_factor + right_part[1] * right_factor
    token_count, head_count = joint_max.shape
    left_rows = left_part[2].reshape(token_count, head_count, HD) * left_factor[..., None]
    right_rows = right_part[2].reshape(token_count, head_count, HD) * right_factor[..., None]
    return (joint_max, weight_sum, (left_rows + right_rows).reshape(left_part[2].shape))


def empty_rims(features):
    return (
        jnp.zeros((HALO, BW, features), jnp.bfloat16),
        jnp.zeros((HALO, BW, features), jnp.bfloat16),
        jnp.zeros((BH, HALO, features), jnp.bfloat16),
        jnp.zeros((BH, HALO, features), jnp.bfloat16),
        jnp.zeros((HALO, HALO, features), jnp.bfloat16),
        jnp.zeros((HALO, HALO, features), jnp.bfloat16),
        jnp.zeros((HALO, HALO, features), jnp.bfloat16),
        jnp.zeros((HALO, HALO, features), jnp.bfloat16),
    )


def pack_rims(block):
    features = block.shape[-1]
    top_band = block[:HALO].reshape(HALO * BW, features)
    bottom_band = block[-HALO:].reshape(HALO * BW, features)
    left_band = block[:, :HALO].reshape(BH * HALO, features)
    right_band = block[:, -HALO:].reshape(BH * HALO, features)
    return jnp.concatenate([top_band, bottom_band, left_band, right_band], axis=0)[None]


def place_rims(tile_map, tile_row, tile_col, totals, packed, start_row):
    piece_count = packed.shape[0]
    features = packed.shape[2]
    row_band = HALO * BW
    col_band = BH * HALO
    top_rows = packed[:, :row_band].reshape(piece_count, HALO, BW, features)
    bottom_rows = packed[:, row_band : 2 * row_band].reshape(piece_count, HALO, BW, features)
    left_cols = packed[:, 2 * row_band : 2 * row_band + col_band].reshape(
        piece_count, BH, HALO, features
    )
    right_cols = packed[:, 2 * row_band + col_band :].reshape(piece_count, BH, HALO, features)
    row_step = tile_map // TX - tile_row
    col_step = tile_map % TX - tile_col

    def select(down, across, source):
        chosen = ((row_step == down) & (col_step == across)).astype(jnp.bfloat16)
        return jnp.einsum("nrcf,n->rcf", source, chosen, preferred_element_type=jnp.float32).astype(
            jnp.bfloat16
        )

    updates = (
        select(-1, 0, bottom_rows),
        select(1, 0, top_rows),
        select(0, -1, right_cols),
        select(0, 1, left_cols),
        select(-1, -1, bottom_rows[:, :, -HALO:]),
        select(-1, 1, bottom_rows[:, :, :HALO]),
        select(1, -1, top_rows[:, :, -HALO:]),
        select(1, 1, top_rows[:, :, :HALO]),
    )
    return tuple((update for update in updates))


def assemble(center, rim_parts):
    north_rim, south_rim, west_rim, east_rim, north_west, north_east, south_west, south_east = (
        rim_parts
    )
    upper_band = jnp.concatenate([north_west, north_rim, north_east], axis=1)
    middle_band = jnp.concatenate([west_rim, center, east_rim], axis=1)
    lower_band = jnp.concatenate([south_west, south_rim, south_east], axis=1)
    return jnp.concatenate([upper_band, middle_band, lower_band], axis=0)


def shards(
    tokens,
    tile_map,
    norm_gain,
    q_weight,
    k_weight,
    v_weight,
    out_weight,
    pos_bias,
    sum_keys,
    sum_values,
):
    feature_share = tokens.shape[3]
    head_share = feature_share // HD
    token_count = BH * BW
    pad_rows = BH + 2 * HALO
    pad_cols = BW + 2 * HALO
    window_span = 2 * HALO + 1
    score_scale = HD ** (-0.5)
    my_tile = tile_map[lax.axis_index("space")]
    tile_row = my_tile // TX
    tile_col = my_tile % TX
    grid_rows = lax.axis_size("space") // TX * BH
    grid_cols = TX * BW
    placer = partial(place_rims, tile_map, tile_row, tile_col)
    gathered = lax.all_gather(tokens, "summ", axis=3, tiled=True)[0]
    normed = normalize(gathered, norm_gain).reshape(token_count, D)
    queries = jnp.dot(normed, q_weight, preferred_element_type=jnp.float32).astype(jnp.bfloat16)
    keys_local = jnp.dot(normed, k_weight, preferred_element_type=jnp.float32).astype(jnp.bfloat16)
    values_local = jnp.dot(normed, v_weight, preferred_element_type=jnp.float32).astype(
        jnp.bfloat16
    )
    paired = jnp.concatenate([keys_local, values_local], axis=-1).reshape(BH, BW, 2 * feature_share)
    rim_parts = placer(
        empty_rims(2 * feature_share),
        lax.all_gather(pack_rims(paired), "space", axis=0, tiled=True),
        jnp.int32(0),
    )
    padded = assemble(paired, rim_parts)
    key_window = padded[..., :feature_share].reshape(pad_rows * pad_cols, head_share, HD)
    value_window = padded[..., feature_share:].reshape(pad_rows * pad_cols, head_share, HD)
    query_heads = queries.reshape(token_count, head_share, HD)
    row_shift = jnp.arange(pad_rows)[None, :] - jnp.arange(BH)[:, None]
    col_shift = jnp.arange(pad_cols)[None, :] - jnp.arange(BW)[:, None]
    row_hot = (row_shift[..., None] == jnp.arange(window_span)).astype(jnp.float32)
    col_hot = (col_shift[..., None] == jnp.arange(window_span)).astype(jnp.float32)
    rel_bias = jnp.einsum(
        "hpq,iap,jbq->ijhab", pos_bias, row_hot, col_hot, precision=lax.Precision.HIGHEST
    )
    rel_bias = rel_bias.reshape(token_count, head_share, pad_rows * pad_cols)
    global_rows = tile_row * BH + jnp.arange(pad_rows) - HALO
    global_cols = tile_col * BW + jnp.arange(pad_cols) - HALO
    near_rows = (
        (row_shift >= 0)
        & (row_shift < window_span)
        & ((global_rows >= 0) & (global_rows < grid_rows))[None, :]
    )
    near_cols = (
        (col_shift >= 0)
        & (col_shift < window_span)
        & ((global_cols >= 0) & (global_cols < grid_cols))[None, :]
    )
    visible = (near_rows[:, None, :, None] & near_cols[None, :, None, :]).reshape(
        token_count, 1, pad_rows * pad_cols
    )
    window_scores = (
        jnp.einsum("thd,khd->thk", query_heads, key_window, preferred_element_type=jnp.float32)
        * score_scale
        + rel_bias
    )
    window_scores = jnp.where(visible, window_scores, -jnp.inf)
    window_max = jnp.max(window_scores, axis=-1)
    window_weights = jnp.exp(window_scores - window_max[..., None])
    window_sum = jnp.sum(window_weights, axis=-1)
    window_weighted = jnp.einsum(
        "thk,khd->thd",
        window_weights.astype(jnp.bfloat16),
        value_window,
        preferred_element_type=jnp.float32,
    )
    all_queries = lax.all_gather(queries, "summ", axis=1, tiled=True)
    partial_max, partial_sum, partial_weighted = summary_heads(
        all_queries, sum_keys, sum_values, D // HD
    )
    merged = combined_all((partial_max, partial_sum, partial_weighted), "summ", merge_parts)
    first_head = lax.axis_index("summ") * head_share
    global_max = lax.dynamic_slice_in_dim(merged[0], first_head, head_share, 1)
    global_sum = lax.dynamic_slice_in_dim(merged[1], first_head, head_share, 1)
    global_weighted = lax.dynamic_slice_in_dim(merged[2], first_head * HD, feature_share, 1)
    joint_max = jnp.maximum(window_max, global_max)
    window_factor = jnp.exp(window_max - joint_max)
    global_factor = jnp.exp(global_max - joint_max)
    weight_sum = window_sum * window_factor + global_sum * global_factor
    weighted = (
        window_weighted * window_factor[..., None]
        + global_weighted.reshape(token_count, head_share, HD) * global_factor[..., None]
    )
    attended = (
        (weighted / weight_sum[..., None]).reshape(token_count, feature_share).astype(jnp.bfloat16)
    )
    head_terms = jnp.dot(attended, out_weight, preferred_element_type=jnp.float32)
    mixed_rows = lax.psum_scatter(
        head_terms.astype(jnp.bfloat16), "summ", scatter_dimension=1, tiled=True
    )
    return mixed_rows.reshape(1, BH, BW, feature_share)


def solution(mesh):
    return jax.shard_map(
        shards,
        mesh=mesh,
        in_specs=(
            P("space", None, None, "summ"),
            P(),
            P(),
            P(None, "summ"),
            P(None, "summ"),
            P(None, "summ"),
            P("summ", None),
            P("summ", None, None),
            P("summ", None),
            P("summ", None),
        ),
        out_specs=P("space", None, None, "summ"),
        check_vma=False,
    )
```

profile of v0, /device:TPU:1, one launch (start us, length us, event | category | flops | bytes accessed | tf_op | source)
XLA Modules:
  0.0 428.4 jit_solution(6247118880206482943)
XLA Ops:
  6.5 21.1 %all_gather.24 = bf16[1,8,32,1024]{3,2,1,0:T(8,128)(2,1)S(1)} all-gather(bf16[1,8,32,128]{3,2,1,0:T(8,128)(2,1)} %param.14), channel_id=1, replica_groups=mesh['space'=64,'summ'=8] {'summ'}, dimensions={3}, use_global_device_ids=true | all-gather | bytes 589824 | tf_op jit(solution)/shard_map/all_gather | solution.py:157
  27.9 0.9 fusion.29
  28.8 1.3 convolution_convert_fusion.1
  30.0 15.0 %all_gather.26 = bf16[256,1024]{0,1:T(8,128)(2,1)S(1)} all-gather(bf16[256,128]{0,1:T(8,128)(2,1)S(1)} %convolution_convert_fusion.1), channel_id=1, replica_groups=mesh['space'=64,'summ'=8] {'summ'}, dimensions={1}, use_global_device_ids=true | all-gather | bytes 589824 | tf_op jit(solution)/shard_map/all_gather | solution.py:212
  45.0 0.5 copy.49
  45.5 1.5 copy.50
  47.0 2.3 copy.51
  49.3 38.0 %while.28 = (s32[]{:T(128)}, f32[16,256]{1,0:T(8,128)S(1)}, f32[16,256]{1,0:T(8,128)S(1)}, f32[16,256,64]{1,2,0:T(8,128)}, bf16[16,256,64]{2,1,0:T(8,128)(2,1)S(...) while((s32[]{:T(128)}, f32[16,256]{1,0:T(8,128)S(1)}, ...), condition=%wide.region_5.6_spmd, body=%wide.region_2.5_spmd.sunk | while | flops 34340352 | bytes 1845349 | solution.py:52
  49.6 1.8 fusion.151
  52.0 1.8 fusion.151
  54.3 1.8 fusion.151
  56.7 1.8 fusion.151
  59.1 1.7 fusion.151
  61.5 1.8 fusion.151
  63.8 1.8 fusion.151
  66.2 1.8 fusion.151
  68.6 1.8 fusion.151
  71.0 1.8 fusion.151
  73.3 1.8 fusion.151
  75.7 1.8 fusion.151
  78.1 1.8 fusion.151
  80.5 1.8 fusion.151
  82.8 1.8 fusion.151
  85.2 1.8 fusion.151
  87.3 2.7 copy.54
  91.4 0.8 copy.40
  92.3 0.6 dynamic_slice.34
  95.4 14.0 %all-gather.1 = f32[2048,16]{0,1:T(8,128)S(1)} all-gather(f32[256,16]{0,1:T(8,128)S(1)} %bitcast.236), channel_id=3, replica_groups=mesh['space'=64,'summ'=8] {'summ'}, dimensions={0}, use_global_device_ids=true | all-gather | bytes 147456 | tf_op jit(solution)/shard_map/all_gather | solution.py:20
  109.4 14.3 %all-gather.2 = f32[2048,16]{0,1:T(8,128)S(1)} all-gather(f32[256,16]{0,1:T(8,128)S(1)} %bitcast.237), channel_id=4, replica_groups=mesh['space'=64,'summ'=8] {'summ'}, dimensions={0}, use_global_device_ids=true | all-gather | bytes 147456 | tf_op jit(solution)/shard_map/all_gather | solution.py:20
  124.3 1.5 and.141
  126.2 3.7 convolution_bitcast_fusion.1
  129.9 5.9 %copy.47 = f32[8,32,2,14,38]{1,0,4,3,2:T(8,128)} copy(f32[8,32,2,14,38]{4,3,1,2,0:T(8,128)} %convolution_bitcast_fusion.1) | data formatting | bytes 2179072 | tf_op jit(solution)/shard_map/hpq,iap,jbq->ijhab/transpose | solution.py:178
  135.8 3.8 reshape.217
  139.7 45.2 %all-gather.6.cloned.1.call-done = f32[8,256,1024]{2,1,0:T(8,128)} async-done(((f32[1,256,1024]{2,1,0:T(8,128)}), f32[8,256,1024]{2,1,0:T(8,128)}) %all-gather.6.cloned.1.call-update) | async-done | bytes 8388624 | tf_op jit(solution)/shard_map/all_gather | solution.py:20
  184.9 1.3 slice_bitcast_fusion
  186.6 7.4 %slice.107 = f32[7,256,1024]{2,1,0:T(8,128)} slice(f32[8,256,1024]{2,1,0:T(8,128)} %all-gather.6.cloned.1.call-done), slice={[1:8], [0:256], [0:1024]} | slice | bytes 14680064 | tf_op jit(solution)/shard_map/slice | solution.py:22
  194.0 23.4 %while.29 = (s32[]{:T(128)}, f32[256,16]{0,1:T(8,128)S(1)}, f32[256,16]{0,1:T(8,128)S(1)}, f32[256,1024]{0,1:T(8,128)S(1)}, f32[7,256,16]{1,0,2:T(8,128)S(1)}, /...) while((s32[]{:T(128)}, f32[256,16]{0,1:T(8,128)S(1)}, f32[256,16]{0,1:T(8,128)S(1)}, ...), condition=%wide.region_7.8_spmd, body=%wide.region_6.7_spmd.sunk | while | flops 811010 | bytes 9404621 | solution.py:23
  194.1 0.6 copy-done.9
  194.8 1.3 constant_dynamic-slice_fusion.7
  196.8 0.5 copy-done.10
  197.4 0.6 copy-done.9
  198.1 1.3 constant_dynamic-slice_fusion.7
  200.2 0.5 copy-done.10
  200.8 0.6 copy-done.9
  201.4 1.3 constant_dynamic-slice_fusion.7
  204.1 0.6 copy-done.9
  204.8 1.3 constant_dynamic-slice_fusion.7
  206.9 0.5 copy-done.10
  207.5 0.6 copy-done.9
  208.1 1.3 constant_dynamic-slice_fusion.7
  210.2 0.5 copy-done.10
  210.8 0.6 copy-done.9
  211.4 1.3 constant_dynamic-slice_fusion.7
  213.5 0.5 copy-done.10
  214.1 0.6 copy-done.9
  214.8 1.3 constant_dynamic-slice_fusion.7
  217.4 154.2 %all-gather.8.cloned.1.call-done = bf16[15360,256]{1,0:T(8,128)(2,1)} async-done(((bf16[240,256]{1,0:T(8,128)(2,1)}), bf16[15360,256]{1,0:T(8,128)(2,1)}) %all-gather.8.cloned.1.call-update) | async-done | bytes 7864336 | tf_op jit(solution)/shard_map/all_gather | solution.py:167
  371.6 3.3 fusion.113
  374.9 1.5 fusion.114
  376.7 1.8 fusion.19
  378.5 1.8 fusion.17
  384.0 1.0 copy.84
  385.0 35.3 %reduce-scatter.4.cloned.1.call-done = bf16[128,256]{1,0:T(8,128)(2,1)} async-done(((bf16[1024,256]{1,0:T(8,128)(2,1)}), bf16[128,256]{1,0:T(8,128)(2,1)}) %reduce-scatter.4.cloned.1.call-update) | async-done | bytes 65552
  420.3 1.6 copy.85
  (232 shorter events, 23.9 us)
Async XLA Ops:
  6.5 377.1 %copy-start = (bf16[128,1024]{1,0:T(8,128)(2,1)S(1)}, bf16[128,1024]{1,0:T(8,128)(2,1)}, u32[]{:S(2)}) copy-start(bf16[128,1024]{1,0:T(8,128)(2,1)} %param.20) | copy-start | bytes 786436
  6.5 178.4 %all-gather.6.cloned.1.call-start = ((), (), s32[]{:S(2)}) async-start(), calls=%async_computation.1 | async-start | bytes 9437184 | tf_op jit(solution)/shard_map/all_gather | solution.py:20
  30.0 15.0 %copy-start.6 = (bf16[256,128]{0,1:T(8,128)(2,1)}, bf16[256,128]{0,1:T(8,128)(2,1)S(1)}, u32[]{:S(2)}) copy-start(bf16[256,128]{0,1:T(8,128)(2,1)S(1)} %convolution_convert_fusion.1) | copy-start | bytes 196612
  87.3 2.8 copy-start.13
  87.3 3.1 copy-start.14
  87.3 5.0 %copy-start.16 = (s32[64]{0:T(128)S(1)}, s32[64]{0:T(128)}, u32[]{:S(2)}) copy-start(s32[64]{0:T(128)} %param.15) | copy-start | bytes 772
  90.0 35.8 %copy-start.15 = (f32[2,7,7]{2,0,1:T(2,128)S(1)}, f32[2,7,7]{2,0,1:T(2,128)}, u32[]{:S(2)}) copy-start(f32[2,7,7]{2,0,1:T(2,128)} %param.21) | copy-start | bytes 1180
  90.0 281.5 %all-gather.8.cloned.1.call-start = ((), (), s32[]{:S(2)}) async-start(), calls=%async_computation.2 | async-start | bytes 7987200 | tf_op jit(solution)/shard_map/all_gather | solution.py:167
  90.9 33.0 %copy-start.2 = (bf16[256,256]{1,0:T(8,128)(2,1)}, bf16[256,256]{1,0:T(8,128)(2,1)S(1)}, u32[]{:S(2)}) copy-start(bf16[256,256]{1,0:T(8,128)(2,1)S(1)} %copy.37) | copy-start | bytes 393220
  92.2 328.1 %reduce-scatter.4.cloned.1.call-start = ((), (), s32[]{:S(2)}) async-start(), calls=%async_computation.3 | async-start | bytes 589824
  109.4 20.5 %copy-start.4 = (f32[2048,16]{0,1:T(8,128)}, f32[2048,16]{0,1:T(8,128)S(1)}, u32[]{:S(2)}) copy-start(f32[2048,16]{0,1:T(8,128)S(1)} %all-gather.1) | copy-start | bytes 393220
  123.8 12.0 %copy-start.5 = (f32[2048,16]{0,1:T(8,128)}, f32[2048,16]{0,1:T(8,128)S(1)}, u32[]{:S(2)}) copy-start(f32[2048,16]{0,1:T(8,128)S(1)} %all-gather.2) | copy-start | bytes 393220
  135.8 3.8 slice-start
  186.6 7.5 %slice-start.1 = ((f32[2048,16]{0,1:T(8,128)}), f32[256,16]{0,1:T(8,128)S(1)}, s32[]{:S(2)}) async-start(f32[2048,16]{0,1:T(8,128)} %copy-done.4), calls=%async_computation.5 | async-start | bytes 32768 | tf_op jit(solution)/shard_map/slice | solution.py:21
  186.6 7.5 %slice-start.2 = ((f32[2048,16]{0,1:T(8,128)}), f32[256,16]{0,1:T(8,128)S(1)}, s32[]{:S(2)}) async-start(f32[2048,16]{0,1:T(8,128)} %copy-done.5), calls=%async_computation.6 | async-start | bytes 32768 | tf_op jit(solution)/shard_map/slice | solution.py:21
  194.0 0.7 copy-start.9
  194.0 0.7 copy-start.11
  196.4 0.9 copy-start.10
  196.4 1.0 copy-start.12
  197.4 0.7 copy-start.9
  197.4 0.7 copy-start.11
  199.7 0.9 copy-start.10
  199.7 1.0 copy-start.12
  200.7 0.7 copy-start.9
  200.7 0.7 copy-start.11
  203.1 0.9 copy-start.10
  203.1 1.0 copy-start.12
  204.0 0.7 copy-start.9
  204.0 0.7 copy-start.11
  206.4 0.9 copy-start.10
  206.4 1.0 copy-start.12
  207.4 0.7 copy-start.9
  207.4 0.7 copy-start.11
  209.7 0.9 copy-start.10
  209.8 1.0 copy-start.12
  210.7 0.7 copy-start.9
  210.7 0.7 copy-start.11
  213.1 0.9 copy-start.10
  213.1 1.0 copy-start.12
  214.1 0.7 copy-start.9
  214.1 0.7 copy-start.11
  216.4 0.9 copy-start.10
  216.4 1.0 copy-start.12
  374.9 1.8 copy-start.17
  380.8 1.4 copy-start.3
  381.1 1.6 copy-start.1
  381.2 1.6 copy-start.7
  381.2 1.6 copy-start.8
Sparse Core Ops, SparseCore 0:
  90.2 94.7 all-gather.5
  189.5 182.0 all-gather.7
  385.1 35.1 reduce-scatter.3
where the time goes:
time: 432 us; the launch traced here: 428 us
  waiting for transfers between devices  235 us (54%)
  blocking collectives  64.4 us (15%)
  local copies, waits for them, and re-layouts  59.4 us (14%)
  matrix products  44.1 us (10%)
  between operations  16.2 us (4%)
  other arithmetic  8.73 us (2%)
    all_gather x1, waiting for transfers between devices, shards(): lax.all_gather(pack_rims(paired), 'space', axis=0, tiled=True)  154 us
    all_gather x1, waiting for transfers between devices, combined_all(): pieces = jax.tree.map(lambda part: lax.all_gather(part, axis), value)  45.2 us
    unnamed x4, waiting for transfers between devices  35.4 us
    all_gather x2, blocking collectives, combined_all(): pieces = jax.tree.map(lambda part: lax.all_gather(part, axis), value)  28.3 us
    dot_general x16, matrix products, summary_part(): jnp.dot(weights.astype(jnp.bfloat16), value_rows, preferred_element_type=...  28.1 us
    all_gather x1, blocking collectives, shards(): gathered = lax.all_gather(tokens, 'summ', axis=3, tiled=True)[0]  21.1 us
    all_gather x1, blocking collectives, shards(): all_queries = lax.all_gather(queries, 'summ', axis=1, tiled=True)  15 us
    dynamic_slice x21, local copies, waits for them, and re-layouts, combined_all(): lax.scan(lambda so_far, slab: (join(so_far, slab), None), head, tail)  11.6 us
  transfers between devices with their start and end apart: 3, of which 3 were waited for; matrix products, arithmetic and copies ran while one was open for 10% of the time, Pallas kernels for 0%

commit v1 on v0

v1 whole, which is shorter than its diff:
```python
from functools import partial

import numpy as np
import jax
import jax.numpy as jnp
from jax import lax
from jax.experimental import pallas as pl
from jax.experimental.pallas import tpu as pltpu
from jax.sharding import PartitionSpec as P

D = 1024
HD = 64
HALO = 3
TX = 8
BW = 32
BH = 8
EPSILON = 1e-05
WIN = 2 * HALO + 1
TOK = BH * BW
LANES = 128
X = 4
YH = 2
YL = 4
CORES = 2
HIDDEN = -1e30
UNIT = 16
UNIT_STEP = (
    [(-1, 0)] * 6
    + [(1, 0)] * 6
    + [(0, -1)] * 2
    + [(0, 1)] * 2
    + [(-1, -1), (-1, 1), (1, -1), (1, 1)]
)
N_UNIT = len(UNIT_STEP)
HALO_KEYS = N_UNIT * UNIT
BAND = HALO * BW
SIDE_ROWS = HALO_KEYS - 2 * BAND
ROUTER_STRIDE = 3
MESH = pl.DeviceIdType.MESH


def halo_positions():
    places = [(-HALO + j // BW, j % BW, (BH - HALO) * BW + j) for j in range(BAND)]
    places += [(BH + j // BW, j % BW, j) for j in range(BAND)]

    def side(count, rows, padded, row_at, col_at, from_row, from_col):
        out = []
        for i in range(padded):
            r, c = i // HALO, i % HALO
            out.append((row_at + r, col_at + c, (from_row + r) * BW + from_col + c) if i < count else None)
        return out

    places += side(BH * HALO, BH, 2 * UNIT, 0, -HALO, 0, BW - HALO)
    places += side(BH * HALO, BH, 2 * UNIT, 0, BW, 0, 0)
    places += side(HALO * HALO, HALO, UNIT, -HALO, -HALO, BH - HALO, BW - HALO)
    places += side(HALO * HALO, HALO, UNIT, -HALO, BW, BH - HALO, 0)
    places += side(HALO * HALO, HALO, UNIT, BH, -HALO, 0, BW - HALO)
    places += side(HALO * HALO, HALO, UNIT, BH, BW, 0, 0)
    return places


def offset_codes():
    keys = [(k // BW, k % BW) for k in range(TOK)]
    keys += [(None if place is None else place[:2]) for place in halo_positions()]
    codes = np.full((len(keys), TOK), -1, np.int32)
    rows, cols = np.arange(TOK) // BW, np.arange(TOK) % BW
    for at, key in enumerate(keys):
        if key is None:
            continue
        i, j = key[0] - rows + HALO, key[1] - cols + HALO
        near = (i >= 0) & (i < WIN) & (j >= 0) & (j < WIN)
        codes[at] = np.where(near, i * WIN + j, -1)
    return codes


def side_picks():
    picks = np.zeros((SIDE_ROWS, TOK), np.float32)
    for at, place in enumerate(halo_positions()[2 * BAND :]):
        if place is not None:
            picks[at, place[2]] = 1.0
    return picks


def kernel(
    n_space,
    tile_map,
    pos_bias,
    tokens,
    gain,
    q_weight,
    k_weight,
    v_weight,
    out_weight,
    sum_keys,
    sum_values,
    codes_in,
    picks_in,
    out,
    gathered,
    normed,
    weights,
    out_w,
    codes,
    picks,
    bias,
    own_k,
    keys,
    values,
    values_t,
    queries,
    part_out,
    part_in,
    stat_out,
    stat_in,
    inverse,
    inverse_s,
    pack,
    routed,
    staged,
    halo,
    terms,
    pair_in,
    pair_sum,
    line_in,
    load_sem,
    inverse_sem,
    tok_send,
    tok_recv,
    k_send,
    k_recv,
    v_send,
    v_recv,
    q_send,
    q_recv,
    part_send,
    part_recv,
    stat_send,
    stat_recv,
    rim_send,
    rim_recv,
    halo_send,
    halo_recv,
    pair_send,
    pair_recv,
    line_send,
    line_recv,
):
    slots = routed.shape[0]
    share = keys.shape[1]
    ty = n_space // TX
    me = lax.axis_index("space")
    my_summ = lax.axis_index("summ")
    y_lo, core = my_summ // CORES, my_summ % CORES
    x_at = me % X
    y_hi = (me // X) % YH
    z_at = me // (X * YH)
    y_at = y_hi * YL + y_lo
    sibling = y_lo * CORES + 1 - core

    def local(src, dst, sem):
        return pltpu.make_async_copy(src, dst, sem)

    def remote(src, dst, send, recv, space, summ):
        return pltpu.make_async_remote_copy(
            src_ref=src,
            dst_ref=dst,
            send_sem=send,
            recv_sem=recv,
            device_id=(space, summ),
            device_id_type=MESH,
        )

    def ring(step, to_core):
        y = (y_at + step + YH * YL) % (YH * YL)
        return (z_at * YH + y // YL) * X + x_at, (y % YL) * CORES + to_core

    def line(step):
        return (y_lo + step) % YL

    loads = [
        local(q_weight, weights.at[:, 0:LANES], load_sem.at[0]),
        local(k_weight, weights.at[:, LANES : 2 * LANES], load_sem.at[1]),
        local(v_weight, weights.at[:, 2 * LANES : 3 * LANES], load_sem.at[2]),
        local(out_weight, out_w, load_sem.at[3]),
        local(codes_in, codes, load_sem.at[4]),
        local(picks_in, picks, load_sem.at[5]),
    ]
    own_tokens = local(tokens, gathered.at[my_summ], tok_recv.at[my_summ])
    own_tokens.start()
    my_rows = pl.ds(pl.multiple_of(x_at * share, share), share)
    my_cols = pl.ds(pl.multiple_of(my_summ * LANES, LANES), LANES)
    local(sum_keys.at[my_rows, my_cols], keys.at[my_summ], k_recv).start()
    local(sum_values.at[my_rows, my_cols], values.at[my_summ], v_recv).start()

    barrier = pltpu.get_barrier_semaphore()

    def greet(space, summ):
        pl.semaphore_signal(barrier, inc=1, device_id=(space, summ), device_id_type=MESH)

    greet(me, sibling)
    for step in range(1, YL):
        greet(me, line(step) * CORES + core)
    for step in (1, -1, 2, -2):
        for to_core in range(CORES):
            greet(*ring(step, to_core))

    def greet_space(step, carry):
        greet((me + step) % n_space, my_summ)
        return carry

    lax.fori_loop(1, n_space, greet_space, 0)
    for load in loads:
        load.start()
    pl.semaphore_wait(barrier, 1 + (YL - 1) + 4 * CORES + n_space - 1)

    sends = []
    for at, step in enumerate((2, 1, 3)):
        sends.append(
            remote(
                tokens,
                gathered.at[my_summ],
                tok_send.at[at],
                tok_recv.at[my_summ],
                me,
                line(step) * CORES + core,
            )
        )
    sends.append(
        remote(tokens, gathered.at[my_summ], tok_send.at[3], tok_recv.at[my_summ], me, sibling)
    )
    for send in sends:
        send.start()

    def give(source, held, send_sem, recv_sem, space, summ):
        cols = pl.ds(pl.multiple_of(summ * LANES, LANES), LANES)
        remote(source.at[my_rows, cols], held.at[my_summ], send_sem, recv_sem, space, summ).start()

    def give_summary():
        for step in (1, -1):
            for to_core in range(CORES):
                give(sum_keys, keys, k_send, k_recv, *ring(step, to_core))
        for to_core in range(CORES):
            give(sum_keys, keys, k_send, k_recv, *ring(2, to_core))
        give(sum_keys, keys, k_send, k_recv, me, sibling)
        for step in (1, -1):
            for to_core in range(CORES):
                give(sum_values, values, v_send, v_recv, *ring(step, to_core))
        for to_core in range(CORES):
            give(sum_values, values, v_send, v_recv, *ring(-2, to_core))
        give(sum_values, values, v_send, v_recv, me, sibling)

    lane = lax.broadcasted_iota(jnp.int32, inverse.shape, 1)

    def place(at, so_far):
        return so_far + jnp.where(lane == tile_map[at], at, 0)

    inverse[...] = lax.fori_loop(0, n_space, place, jnp.zeros(inverse.shape, jnp.int32))
    to_scalars = local(inverse, inverse_s, inverse_sem)
    to_scalars.start()

    loads[4].wait()

    def fill(at, carry):
        rows = pl.ds(pl.multiple_of(at * UNIT, UNIT), UNIT)
        code = codes[rows, :]
        first = jnp.full(code.shape, HIDDEN, jnp.float32)
        second = first
        for i in range(WIN):
            for j in range(WIN):
                here = code == i * WIN + j
                first = jnp.where(here, pos_bias[0, i, j], first)
                second = jnp.where(here, pos_bias[1, i, j], second)
        bias[0, rows, :] = first
        bias[1, rows, :] = second
        return carry

    lax.fori_loop(0, bias.shape[1] // UNIT, fill, 0)
    my_tile = tile_map[me]
    tile_row, tile_col = my_tile // TX, my_tile % TX
    edge = {
        (-1, 0): jnp.where(tile_row > 0, 0.0, HIDDEN),
        (1, 0): jnp.where(tile_row < ty - 1, 0.0, HIDDEN),
        (0, -1): jnp.where(tile_col > 0, 0.0, HIDDEN),
        (0, 1): jnp.where(tile_col < TX - 1, 0.0, HIDDEN),
    }
    for down in (-1, 1):
        for across in (-1, 1):
            edge[down, across] = jnp.minimum(edge[down, 0], edge[0, across])
    for step, hidden in edge.items():
        at = TOK + UNIT_STEP.index(step) * UNIT
        rows = slice(at, at + UNIT_STEP.count(step) * UNIT)
        for h in range(2):
            bias[h, rows, :] = bias[h, rows, :] + hidden

    forwards = []
    for at, step in enumerate((1, 3, 2)):
        slab = line(step) * CORES + core
        local(gathered.at[slab], gathered.at[slab], tok_recv.at[slab]).wait()
        forward = remote(
            gathered.at[slab],
            gathered.at[slab],
            tok_send.at[4 + at],
            tok_recv.at[slab],
            me,
            sibling,
        )
        forward.start()
        forwards.append(forward)
    own_tokens.wait()
    for step in range(YL):
        slab = line(step) * CORES + 1 - core
        local(gathered.at[slab], gathered.at[slab], tok_recv.at[slab]).wait()
    give_summary()

    squares = jnp.zeros((TOK, LANES), jnp.float32)
    for slab in range(YL * CORES):
        floats = gathered[slab].astype(jnp.float32)
        squares = squares + floats * floats
    scale = lax.rsqrt(jnp.sum(squares, axis=-1, keepdims=True) * (1.0 / D) + EPSILON)
    for slab in range(YL * CORES):
        cols = slice(slab * LANES, (slab + 1) * LANES)
        floats = gathered[slab].astype(jnp.float32)
        normed[:, cols] = (floats * scale * gain[:, cols]).astype(jnp.bfloat16)
    for load in loads[:3]:
        load.wait()
    projected = jnp.dot(normed[...], weights[...], preferred_element_type=jnp.float32)
    projected = projected.astype(jnp.bfloat16)
    own_k[...] = projected[:, LANES : 2 * LANES]
    own_v = projected[:, 2 * LANES :]

    loads[5].wait()
    sides = jnp.dot(picks[...], projected[:, LANES:], preferred_element_type=jnp.float32)
    sides = sides.astype(jnp.bfloat16)
    for which in range(2):
        own = projected[:, (1 + which) * LANES : (2 + which) * LANES]
        first = which * N_UNIT
        bands = BAND // UNIT
        pack[first : first + bands] = own[TOK - BAND :].reshape(bands, UNIT, LANES)
        pack[first + bands : first + 2 * bands] = own[:BAND].reshape(bands, UNIT, LANES)
        pack[first + 2 * bands : first + N_UNIT] = sides[
            :, which * LANES : (which + 1) * LANES
        ].reshape(N_UNIT - 2 * bands, UNIT, LANES)

    def send_rim(unit, carry):
        router = (unit * ROUTER_STRIDE) % n_space
        slot = unit // n_space

        @pl.when(router != me)
        def _():
            remote(
                pack.at[unit],
                routed.at[slot, me],
                rim_send,
                rim_recv.at[slot],
                router,
                my_summ,
            ).start()

        @pl.when(router == me)
        def _():
            local(pack.at[unit], routed.at[slot, me], rim_recv.at[slot]).start()

        return carry

    lax.fori_loop(0, 2 * N_UNIT, send_rim, 0)

    scaled = projected[:, :LANES].astype(jnp.float32) * HD ** (-0.5)
    queries[x_at] = scaled.T.astype(jnp.bfloat16)
    peers = [(x_at + step) % X for step in range(X)]
    for step in range(1, X):
        remote(
            queries.at[x_at],
            queries.at[x_at],
            q_send,
            q_recv.at[x_at],
            me - x_at + peers[step],
            my_summ,
        ).start()

    def one_head(both, h):
        blank = jnp.zeros((HD, TOK), jnp.bfloat16)
        own = both[h * HD : (h + 1) * HD]
        return jnp.concatenate([own, blank] if h == 0 else [blank, own], axis=0)

    def attend(scores, v_rows):
        top = jnp.max(scores, axis=0, keepdims=True)
        weight = jnp.exp(scores - top)
        total = jnp.sum(weight, axis=0, keepdims=True)
        summed = jnp.dot(v_rows, weight.astype(jnp.bfloat16), preferred_element_type=jnp.float32)
        return top, total, summed

    my_queries = queries[x_at]
    own_vt = own_v.astype(jnp.float32).T.astype(jnp.bfloat16)
    parts = [[], []]
    for h in range(2):
        scores = jnp.dot(own_k[...], one_head(my_queries, h), preferred_element_type=jnp.float32)
        parts[h].append(attend(scores + bias[h, :TOK], own_vt[h * HD : (h + 1) * HD]))

    to_scalars.wait()
    first_unit = (me * pow(ROUTER_STRIDE, -1, n_space)) % n_space
    for slot in range(slots):
        unit = first_unit + slot * n_space

        @pl.when(unit < 2 * N_UNIT)
        def _():
            local(routed.at[slot], routed.at[slot], rim_recv.at[slot]).wait()
            kind = unit % N_UNIT
            down = jnp.where(
                kind < 6, -1, jnp.where(kind < 12, 1, jnp.where(kind < 16, 0, jnp.where(kind < 18, -1, 1)))
            )
            across = jnp.where(
                kind < 12,
                0,
                jnp.where(kind < 14, -1, jnp.where(kind < 16, 1, jnp.where(kind % 2 == 0, -1, 1))),
            )

            def pass_on(to, carry):
                tile = tile_map[to]
                row = jnp.clip(tile // TX + down, 0, ty - 1)
                col = jnp.clip(tile % TX + across, 0, TX - 1)
                holder = jnp.clip(inverse_s[0, row * TX + col], 0, n_space - 1)
                staged[slot, to] = routed[slot, holder]

                @pl.when(to != me)
                def _():
                    remote(
                        staged.at[slot, to], halo.at[unit], halo_send, halo_recv, to, my_summ
                    ).start()

                @pl.when(to == me)
                def _():
                    local(staged.at[slot, to], halo.at[unit], halo_recv).start()

                return carry

            lax.fori_loop(0, n_space, pass_on, 0)

    local(values, values, v_recv).wait()
    for slab in range(YL * CORES):
        values_t[:, slab * share : (slab + 1) * share] = (
            values[slab].astype(jnp.float32).T.astype(jnp.bfloat16)
        )
    local(keys, keys, k_recv).wait()

    def summary(step, carry):
        peer = (x_at + step) % X

        @pl.when(step > 0)
        def _():
            local(queries.at[peer], queries.at[peer], q_recv.at[peer]).wait()

        theirs = queries[peer]
        key_rows = keys[...].reshape(YL * CORES * share, LANES)
        tops, totals, sums = [], [], []
        for h in range(2):
            scores = jnp.dot(key_rows, one_head(theirs, h), preferred_element_type=jnp.float32)
            top, total, summed = attend(scores, values_t[h * HD : (h + 1) * HD, :])
            tops.append(top)
            totals.append(total)
            sums.append(summed)
        part_out[peer] = jnp.concatenate(sums, axis=0).astype(jnp.bfloat16)
        stat_out[peer] = jnp.concatenate(tops + totals + [jnp.zeros((4, TOK), jnp.float32)], axis=0)

        @pl.when(step > 0)
        def _():
            to = me - x_at + peer
            remote(
                part_out.at[peer], part_in.at[x_at], part_send, part_recv.at[x_at], to, my_summ
            ).start()
            remote(
                stat_out.at[peer], stat_in.at[x_at], stat_send, stat_recv.at[x_at], to, my_summ
            ).start()

        return carry

    lax.fori_loop(0, X, summary, 0)

    local(halo, halo, halo_recv).wait()
    halo_k = halo[:N_UNIT].reshape(HALO_KEYS, LANES)
    halo_vt = halo[N_UNIT:].reshape(HALO_KEYS, LANES).astype(jnp.float32).T.astype(jnp.bfloat16)
    for h in range(2):
        scores = jnp.dot(halo_k, one_head(my_queries, h), preferred_element_type=jnp.float32)
        parts[h].append(attend(scores + bias[h, TOK:], halo_vt[h * HD : (h + 1) * HD]))

    for step in range(X):
        peer = peers[step]
        if step > 0:
            local(part_in.at[peer], part_in.at[peer], part_recv.at[peer]).wait()
            local(stat_in.at[peer], stat_in.at[peer], stat_recv.at[peer]).wait()
            rows, stats = part_in[peer], stat_in[peer]
        else:
            rows, stats = part_out[peer], stat_out[peer]
        for h in range(2):
            parts[h].append(
                (
                    stats[h : h + 1],
                    stats[2 + h : 3 + h],
                    rows[h * HD : (h + 1) * HD].astype(jnp.float32),
                )
            )
    heads = []
    for h in range(2):
        joint = parts[h][0][0]
        for top, _, _ in parts[h][1:]:
            joint = jnp.maximum(joint, top)
        total = jnp.zeros((1, TOK), jnp.float32)
        summed = jnp.zeros((HD, TOK), jnp.float32)
        for top, part_total, part_sum in parts[h]:
            factor = jnp.exp(top - joint)
            total = total + part_total * factor
            summed = summed + part_sum * factor
        heads.append(summed / total)
    attended = jnp.concatenate(heads, axis=0).T.astype(jnp.bfloat16)

    loads[3].wait()
    mixed = jnp.dot(attended, out_w[...], preferred_element_type=jnp.float32).astype(jnp.bfloat16)
    for at in range(YL):
        for side in range(CORES):
            slab = at * CORES + side
            terms[side, at] = mixed[:, slab * LANES : (slab + 1) * LANES]
    order = [line(step) for step in (2, 1, 3, 0)]
    pair = []
    for at in order:
        pair.append(
            remote(
                terms.at[1 - core, at], pair_in.at[at], pair_send.at[at], pair_recv.at[at], me, sibling
            )
        )
        pair[-1].start()
    along = []
    for at in order[:3]:
        local(pair_in.at[at], pair_in.at[at], pair_recv.at[at]).wait()
        both = terms[core, at].astype(jnp.float32) + pair_in[at].astype(jnp.float32)
        pair_sum[at] = both.astype(jnp.bfloat16)
        along.append(
            remote(
                pair_sum.at[at],
                line_in.at[y_lo],
                line_send.at[at],
                line_recv.at[y_lo],
                me,
                at * CORES + core,
            )
        )
        along[-1].start()
    local(pair_in.at[y_lo], pair_in.at[y_lo], pair_recv.at[y_lo]).wait()
    result = terms[core, y_lo].astype(jnp.float32) + pair_in[y_lo].astype(jnp.float32)
    for step in (1, 3, 2):
        at = line(step)
        local(line_in.at[at], line_in.at[at], line_recv.at[at]).wait()
        result = result + line_in[at].astype(jnp.float32)
    out[...] = result.astype(jnp.bfloat16)

    for send in sends + forwards + pair + along:
        send.wait_send()
    for sem, held in ((k_send, keys), (v_send, values)):
        sent = held.at[: YL * CORES - 1]
        local(sent, sent, sem).wait()
    for sem, held in ((q_send, queries), (part_send, part_out), (stat_send, stat_out)):
        sent = held.at[: X - 1]
        local(sent, sent, sem).wait()
    routers = [(unit * ROUTER_STRIDE) % n_space for unit in range(2 * N_UNIT)]
    own_units = jnp.where(first_unit < (2 * N_UNIT) % n_space, 1, 0) + 2 * N_UNIT // n_space
    for count in sorted({routers.count(at) for at in range(n_space)}):

        @pl.when(own_units == count)
        def _():
            sent = pack.at[: 2 * N_UNIT - count]
            local(sent, sent, rim_send).wait()

    for slot in range(slots):

        @pl.when(first_unit + slot * n_space < 2 * N_UNIT)
        def _():
            sent = staged.at[slot, : n_space - 1]
            local(sent, sent, halo_send).wait()


def shards(
    n_space,
    tokens,
    tile_map,
    norm_gain,
    q_weight,
    k_weight,
    v_weight,
    out_weight,
    pos_bias,
    sum_keys,
    sum_values,
):
    share = sum_keys.shape[0] // X
    slots = -(-2 * N_UNIT // n_space)
    bf16 = jnp.bfloat16
    f32 = jnp.float32
    dma = pltpu.SemaphoreType.DMA
    anywhere = pl.BlockSpec(memory_space=pl.ANY)
    scalars = pl.BlockSpec(memory_space=pltpu.SMEM)
    vector = pl.BlockSpec(memory_space=pltpu.VMEM)
    slab = (TOK, LANES)
    turned = (LANES, TOK)
    scratch = [
        pltpu.VMEM((YL * CORES,) + slab, bf16),
        pltpu.VMEM((TOK, D), bf16),
        pltpu.VMEM((D, 3 * LANES), bf16),
        pltpu.VMEM((LANES, D), bf16),
        pltpu.VMEM((TOK + HALO_KEYS, TOK), jnp.int32),
        pltpu.VMEM((SIDE_ROWS, TOK), bf16),
        pltpu.VMEM((2, TOK + HALO_KEYS, TOK), f32),
        pltpu.VMEM(slab, bf16),
        pltpu.VMEM((YL * CORES, share, LANES), bf16),
        pltpu.VMEM((YL * CORES, share, LANES), bf16),
        pltpu.VMEM((LANES, YL * CORES * share), bf16),
        pltpu.VMEM((X,) + turned, bf16),
        pltpu.VMEM((X,) + turned, bf16),
        pltpu.VMEM((X,) + turned, bf16),
        pltpu.VMEM((X, 8, TOK), f32),
        pltpu.VMEM((X, 8, TOK), f32),
        pltpu.VMEM((8, LANES), jnp.int32),
        pltpu.SMEM((8, LANES), jnp.int32),
        pltpu.VMEM((2 * N_UNIT, UNIT, LANES), bf16),
        pltpu.VMEM((slots, n_space, UNIT, LANES), bf16),
        pltpu.VMEM((slots, n_space, UNIT, LANES), bf16),
        pltpu.VMEM((2 * N_UNIT, UNIT, LANES), bf16),
        pltpu.VMEM((CORES, YL) + slab, bf16),
        pltpu.VMEM((YL,) + slab, bf16),
        pltpu.VMEM((YL,) + slab, bf16),
        pltpu.VMEM((YL,) + slab, bf16),
        dma((6,)),
        dma,
        dma((7,)),
        dma((YL * CORES,)),
        dma,
        dma,
        dma,
        dma,
        dma,
        dma((X,)),
        dma,
        dma((X,)),
        dma,
        dma((X,)),
        dma,
        dma((slots,)),
        dma,
        dma,
        dma((YL,)),
        dma((YL,)),
        dma((YL,)),
        dma((YL,)),
    ]
    mixed = pl.pallas_call(
        partial(kernel, n_space),
        out_shape=jax.ShapeDtypeStruct(slab, bf16),
        in_specs=[scalars, scalars, anywhere, vector] + [anywhere] * 8,
        out_specs=vector,
        scratch_shapes=scratch,
        compiler_params=pltpu.CompilerParams(
            collective_id=0, has_side_effects=True, vmem_limit_bytes=48 * 1024 * 1024
        ),
        name="tile_attention",
    )(
        tile_map,
        pos_bias,
        tokens.reshape(slab),
        norm_gain.reshape(1, D),
        q_weight,
        k_weight,
        v_weight,
        out_weight,
        sum_keys,
        sum_values,
        jnp.asarray(offset_codes()),
        jnp.asarray(side_picks(), bf16),
    )
    return mixed.reshape(1, BH, BW, LANES)


def solution(mesh):
    return jax.shard_map(
        partial(shards, mesh.shape["space"]),
        mesh=mesh,
        in_specs=(
            P("space", None, None, "summ"),
            P(),
            P(),
            P(None, "summ"),
            P(None, "summ"),
            P(None, "summ"),
            P("summ", None),
            P("summ", None, None),
            P("summ", None),
            P("summ", None),
        ),
        out_specs=P("space", None, None, "summ"),
        check_vma=False,
    )
```

time: 432 us -> 72.3 us (0.17)
  waiting for transfers between devices: 235 us -> 0 us
  blocking collectives: 64.4 us -> 0 us
  Pallas kernels: 0 us -> 61.4 us
  local copies, waits for them, and re-layouts: 59.4 us -> 10.3 us
  matrix products: 44.1 us -> 0 us
  between operations: 16.2 us -> 0.02 us
  other arithmetic: 8.73 us -> 0 us
    all_gather x2 -> x0, waiting for transfers between devices: 199 us -> none  [the longest x1 154 us: shards(): lax.all_gather(pack_rims(paired), 'space', axis=0, tiled=True)]
    all_gather x4 -> x0, blocking collectives: 64.4 us -> none  [the longest x2 28.3 us: combined_all(): pieces = jax.tree.map(lambda part: lax.all_gather(part, axis), value)]
    pallas_call x0 -> x1, Pallas kernels: none -> 61.4 us  [shards(): pl.pallas_call(partial(kernel, n_space), out_shape=jax.ShapeDtypeStruct(s...]
    dot_general x48 -> x0, matrix products: 44.1 us -> none  [the longest x16 28.1 us: summary_part(): jnp.dot(weights.astype(jnp.bfloat16), value_rows, preferred_element_type=...]
    unnamed x4 -> x0, waiting for transfers between devices: 35.4 us -> none
    slice x18 -> x0, local copies, waits for them, and re-layouts: 13.4 us -> none  [the longest x6 7.52 us: combined_all(): tail = jax.tree.map(lambda part: part[1:], pieces)]
    dynamic_slice x23 -> x0, local copies, waits for them, and re-layouts: 12.3 us -> none  [the longest x21 11.6 us: combined_all(): lax.scan(lambda so_far, slab: (join(so_far, slab), None), head, tail)]
    while x57 -> x0, local copies, waits for them, and re-layouts: 8.62 us -> none
  transfers between devices with their start and end apart: 3 -> 0, of which waited for: 3 -> 0; matrix products, arithmetic and copies ran while one was open for 10% -> 0% of each run, Pallas kernels for 0% -> 0%
where the time goes in v1:
time: 72.3 us; the launch traced here: 71.8 us
  Pallas kernels  61.4 us (85%)
  local copies, waits for them, and re-layouts  10.3 us (14%)
    pallas_call x1, Pallas kernels, shards(): pl.pallas_call(partial(kernel, n_space), out_shape=jax.ShapeDtypeStruct(s...  61.4 us
    unnamed x24, local copies, waits for them, and re-layouts  10.3 us

profile of v1, /device:TPU:1, one launch (start us, length us, event | category | flops | bytes accessed | tf_op | source)
XLA Modules:
  0.0 71.8 jit_solution(1699724029250446658)
XLA Ops:
  0.0 0.0 copy-start.9
  0.0 0.0 copy-start.10
  0.0 0.7 %copy.13.pos_bias = f32[2,7,7]{2,1,0:T(8,128)S(1)} copy(f32[2,7,7]{2,0,1:T(2,128)} %param.19) | data formatting | bytes 784 | tf_op args[7]
  0.7 0.0 copy-done.9
  0.7 0.0 copy-done.10
  0.7 0.0 copy-start
  0.7 1.2 %copy-done = bf16[512,1024]{1,0:T(8,128)(2,1)S(1)} copy-done((bf16[512,1024]{1,0:T(8,128)(2,1)S(1)}, bf16[512,1024]{1,0:T(8,128)(2,1)}, u32[]{:S(2)}) %copy-start) | copy-done | bytes 1048600
  2.0 0.0 copy-start.1
  2.0 1.2 %copy-done.1 = bf16[512,1024]{1,0:T(8,128)(2,1)S(1)} copy-done((bf16[512,1024]{1,0:T(8,128)(2,1)S(1)}, bf16[512,1024]{1,0:T(8,128)(2,1)}, u32[]{:S(2)}) %copy-start.1) | copy-done | bytes 1048600
  3.2 0.0 copy-start.2
  3.2 1.1 %copy-done.2 = s32[576,256]{1,0:T(8,128)S(1)} copy-done((s32[576,256]{1,0:T(8,128)S(1)}, s32[576,256]{1,0:T(8,128)}, u32[]{:S(2)}) %copy-start.2) | copy-done | bytes 589848
  4.2 0.0 copy-start.3
  4.3 0.9 %copy-done.3 = bf16[1024,128]{1,0:T(8,128)(2,1)S(1)} copy-done((bf16[1024,128]{1,0:T(8,128)(2,1)S(1)}, bf16[1024,128]{1,0:T(8,128)(2,1)}, u32[]{:S(2)}) %copy-start.3) | copy-done | bytes 262168
  5.2 0.0 copy-start.4
  5.2 0.9 %copy-done.4 = bf16[1024,128]{1,0:T(8,128)(2,1)S(1)} copy-done((bf16[1024,128]{1,0:T(8,128)(2,1)S(1)}, bf16[1024,128]{1,0:T(8,128)(2,1)}, u32[]{:S(2)}) %copy-start.4) | copy-done | bytes 262168
  6.2 0.0 copy-start.5
  6.2 0.9 %copy-done.5 = bf16[1024,128]{1,0:T(8,128)(2,1)S(1)} copy-done((bf16[1024,128]{1,0:T(8,128)(2,1)S(1)}, bf16[1024,128]{1,0:T(8,128)(2,1)}, u32[]{:S(2)}) %copy-start.5) | copy-done | bytes 262168
  7.1 0.0 copy-start.6
  7.1 0.9 %copy-done.6 = bf16[128,1024]{1,0:T(8,128)(2,1)S(1)} copy-done((bf16[128,1024]{1,0:T(8,128)(2,1)S(1)}, bf16[128,1024]{1,0:T(8,128)(2,1)}, u32[]{:S(2)}) %copy-start.6) | copy-done | bytes 262168
  8.1 0.0 copy-start.7
  8.1 0.8 %copy-done.7 = bf16[1,8,32,128]{3,2,1,0:T(8,128)(2,1)S(1)} copy-done((bf16[1,8,32,128]{3,2,1,0:T(8,128)(2,1)S(1)}, bf16[1,8,32,128]{3,2,1,0:T(8,128)(2,1)}, u32[]{:S(2)}) %copy-start.7) | copy-done | bytes 65560
  8.9 0.0 copy-start.8
  8.9 0.8 %copy-done.8 = bf16[128,256]{1,0:T(8,128)(2,1)S(1)} copy-done((bf16[128,256]{1,0:T(8,128)(2,1)S(1)}, bf16[128,256]{1,0:T(8,128)(2,1)}, u32[]{:S(2)}) %copy-start.8) | copy-done | bytes 65560
  9.7 61.4 %tile_attention.1 = bf16[256,128]{1,0:T(8,128)(2,1)S(1)} custom-call(s32[64]{0:T(128)S(1)} %copy-done.10, f32[2,7,7]{2,1,0:T(8,128)S(1)} %copy.13.pos_bias, bf16[256,128]{1,0:T(8,128)(2,1)S(1)} %bitcast.4, f32[1,1024]{1,0:T(1,128)S(1)} %bitcast.5, bf16[1024,128]{1,0:T(8,128)(2,1)S(1)} %copy-done.3, bf16[1024,128]{1,0:T(8,128)(2,1)S(1)} %copy-done.4, ...), custom_call_target="tpu_custom_call" | custom-call | tf_op jit(solution)/shard_map/tile_attention/pallas_call | solution.py:652
  71.1 0.6 copy.15
Async XLA Ops:
  0.0 0.7 %copy-start.9 = (f32[1024]{0:T(1024)S(1)}, f32[1024]{0:T(1024)}, u32[]{:S(2)}) copy-start(f32[1024]{0:T(1024)} %param.14) | copy-start | bytes 12292
  0.0 0.7 %copy-start.10 = (s32[64]{0:T(128)S(1)}, s32[64]{0:T(128)}, u32[]{:S(2)}) copy-start(s32[64]{0:T(128)} %tile_map.1) | copy-start | bytes 772
  0.7 1.2 %copy-start = (bf16[512,1024]{1,0:T(8,128)(2,1)S(1)}, bf16[512,1024]{1,0:T(8,128)(2,1)}, u32[]{:S(2)}) copy-start(bf16[512,1024]{1,0:T(8,128)(2,1)} %sum_keys.1) | copy-start | bytes 3145732
  2.0 1.2 %copy-start.1 = (bf16[512,1024]{1,0:T(8,128)(2,1)S(1)}, bf16[512,1024]{1,0:T(8,128)(2,1)}, u32[]{:S(2)}) copy-start(bf16[512,1024]{1,0:T(8,128)(2,1)} %sum_values.1) | copy-start | bytes 3145732
  3.2 1.1 %copy-start.2 = (s32[576,256]{1,0:T(8,128)S(1)}, s32[576,256]{1,0:T(8,128)}, u32[]{:S(2)}) copy-start(s32[576,256]{1,0:T(8,128)} %constant.4.clone.codes_in) | copy-start | bytes 1769476
  4.2 0.9 %copy-start.3 = (bf16[1024,128]{1,0:T(8,128)(2,1)S(1)}, bf16[1024,128]{1,0:T(8,128)(2,1)}, u32[]{:S(2)}) copy-start(bf16[1024,128]{1,0:T(8,128)(2,1)} %q_weight.1) | copy-start | bytes 786436
  5.2 0.9 %copy-start.4 = (bf16[1024,128]{1,0:T(8,128)(2,1)S(1)}, bf16[1024,128]{1,0:T(8,128)(2,1)}, u32[]{:S(2)}) copy-start(bf16[1024,128]{1,0:T(8,128)(2,1)} %k_weight.1) | copy-start | bytes 786436
  6.2 0.9 %copy-start.5 = (bf16[1024,128]{1,0:T(8,128)(2,1)S(1)}, bf16[1024,128]{1,0:T(8,128)(2,1)}, u32[]{:S(2)}) copy-start(bf16[1024,128]{1,0:T(8,128)(2,1)} %v_weight.1) | copy-start | bytes 786436
  7.1 0.9 %copy-start.6 = (bf16[128,1024]{1,0:T(8,128)(2,1)S(1)}, bf16[128,1024]{1,0:T(8,128)(2,1)}, u32[]{:S(2)}) copy-start(bf16[128,1024]{1,0:T(8,128)(2,1)} %out_weight.1) | copy-start | bytes 786436
  8.1 0.8 %copy-start.7 = (bf16[1,8,32,128]{3,2,1,0:T(8,128)(2,1)S(1)}, bf16[1,8,32,128]{3,2,1,0:T(8,128)(2,1)}, u32[]{:S(2)}) copy-start(bf16[1,8,32,128]{3,2,1,0:T(8,128)(2,1)} %param.12) | copy-start | bytes 196612
  8.9 0.8 %copy-start.8 = (bf16[128,256]{1,0:T(8,128)(2,1)S(1)}, bf16[128,256]{1,0:T(8,128)(2,1)}, u32[]{:S(2)}) copy-start(bf16[128,256]{1,0:T(8,128)(2,1)} %constant.5.clone.picks_in) | copy-start | bytes 196612

commit v2 on v1

--- a/solution.py
+++ b/solution.py
@@ -35,7 +35,7 @@
 HALO_KEYS = N_UNIT * UNIT
 BAND = HALO * BW
 SIDE_ROWS = HALO_KEYS - 2 * BAND
-ROUTER_STRIDE = 3
+LATE_Z = 5
 MESH = pl.DeviceIdType.MESH
 
 
@@ -146,6 +146,7 @@
     line_recv,
 ):
     slots = routed.shape[0]
+    n_routers = min(n_space, 2 * N_UNIT)
     share = keys.shape[1]
     ty = n_space // TX
     me = lax.axis_index("space")
@@ -204,14 +205,21 @@
         for to_core in range(CORES):
             greet(*ring(step, to_core))
 
+    for step in range(1, X):
+        greet(me - x_at + (x_at + step) % X, my_summ)
+
     def greet_space(step, carry):
         greet((me + step) % n_space, my_summ)
         return carry
 
-    lax.fori_loop(1, n_space, greet_space, 0)
+    @pl.when(me < n_routers)
+    def _():
+        lax.fori_loop(1, n_space, greet_space, 0)
+
     for load in loads:
         load.start()
-    pl.semaphore_wait(barrier, 1 + (YL - 1) + 4 * CORES + n_space - 1)
+    near = 1 + (YL - 1) + 4 * CORES + (X - 1)
+    pl.semaphore_wait(barrier, near + n_routers - jnp.where(me < n_routers, 1, 0))
 
     sends = []
     for at, step in enumerate((2, 1, 3)):
@@ -249,6 +257,10 @@
             give(sum_values, values, v_send, v_recv, *ring(-2, to_core))
         give(sum_values, values, v_send, v_recv, me, sibling)
 
+    @pl.when(z_at < LATE_Z)
+    def _():
+        give_summary()
+
     lane = lax.broadcasted_iota(jnp.int32, inverse.shape, 1)
 
     def place(at, so_far):
@@ -268,8 +280,8 @@
         for i in range(WIN):
             for j in range(WIN):
                 here = code == i * WIN + j
-                first = jnp.where(here, pos_bias[0, i, j], first)
-                second = jnp.where(here, pos_bias[1, i, j], second)
+                first = jnp.where(here, pos_bias[i, 0, j], first)
+                second = jnp.where(here, pos_bias[i, 1, j], second)
         bias[0, rows, :] = first
         bias[1, rows, :] = second
         return carry
@@ -310,7 +322,6 @@
     for step in range(YL):
         slab = line(step) * CORES + 1 - core
         local(gathered.at[slab], gathered.at[slab], tok_recv.at[slab]).wait()
-    give_summary()
 
     squares = jnp.zeros((TOK, LANES), jnp.float32)
     for slab in range(YL * CORES):
@@ -323,16 +334,16 @@
         normed[:, cols] = (floats * scale * gain[:, cols]).astype(jnp.bfloat16)
     for load in loads[:3]:
         load.wait()
-    projected = jnp.dot(normed[...], weights[...], preferred_element_type=jnp.float32)
-    projected = projected.astype(jnp.bfloat16)
-    own_k[...] = projected[:, LANES : 2 * LANES]
-    own_v = projected[:, 2 * LANES :]
+    own_kv = jnp.dot(normed[...], weights[:, LANES:], preferred_element_type=jnp.float32)
+    own_kv = own_kv.astype(jnp.bfloat16)
+    own_k[...] = own_kv[:, :LANES]
+    own_v = own_kv[:, LANES:]
 
     loads[5].wait()
-    sides = jnp.dot(picks[...], projected[:, LANES:], preferred_element_type=jnp.float32)
+    sides = jnp.dot(picks[...].astype(jnp.bfloat16), own_kv, preferred_element_type=jnp.float32)
     sides = sides.astype(jnp.bfloat16)
     for which in range(2):
-        own = projected[:, (1 + which) * LANES : (2 + which) * LANES]
+        own = own_kv[:, which * LANES : (which + 1) * LANES]
         first = which * N_UNIT
         bands = BAND // UNIT
         pack[first : first + bands] = own[TOK - BAND :].reshape(bands, UNIT, LANES)
@@ -342,7 +353,7 @@
         ].reshape(N_UNIT - 2 * bands, UNIT, LANES)
 
     def send_rim(unit, carry):
-        router = (unit * ROUTER_STRIDE) % n_space
+        router = unit % n_space
         slot = unit // n_space
 
         @pl.when(router != me)
@@ -364,7 +375,8 @@
 
     lax.fori_loop(0, 2 * N_UNIT, send_rim, 0)
 
-    scaled = projected[:, :LANES].astype(jnp.float32) * HD ** (-0.5)
+    own_q = jnp.dot(normed[...], weights[:, :LANES], preferred_element_type=jnp.float32)
+    scaled = own_q.astype(jnp.bfloat16).astype(jnp.float32) * HD ** (-0.5)
     queries[x_at] = scaled.T.astype(jnp.bfloat16)
     peers = [(x_at + step) % X for step in range(X)]
     for step in range(1, X):
@@ -396,10 +408,53 @@
         scores = jnp.dot(own_k[...], one_head(my_queries, h), preferred_element_type=jnp.float32)
         parts[h].append(attend(scores + bias[h, :TOK], own_vt[h * HD : (h + 1) * HD]))
 
+    @pl.when(z_at >= LATE_Z)
+    def _():
+        give_summary()
+
+    local(values, values, v_recv).wait()
+    for slab in range(YL * CORES):
+        values_t[:, slab * share : (slab + 1) * share] = (
+            values[slab].astype(jnp.float32).T.astype(jnp.bfloat16)
+        )
+    local(keys, keys, k_recv).wait()
+
+    def summary(step, carry):
+        peer = (x_at + step) % X
+
+        @pl.when(step > 0)
+        def _():
+            local(queries.at[peer], queries.at[peer], q_recv.at[peer]).wait()
+
+        theirs = queries[peer]
+        key_rows = keys[...].reshape(YL * CORES * share, LANES)
+        tops, totals, sums = [], [], []
+        for h in range(2):
+            scores = jnp.dot(key_rows, one_head(theirs, h), preferred_element_type=jnp.float32)
+            top, total, summed = attend(scores, values_t[h * HD : (h + 1) * HD, :])
+            tops.append(top)
+            totals.append(total)
+            sums.append(summed)
+        part_out[peer] = jnp.concatenate(sums, axis=0).astype(jnp.bfloat16)
+        stat_out[peer] = jnp.concatenate(tops + totals + [jnp.zeros((4, TOK), jnp.float32)], axis=0)
+
+        @pl.when(step > 0)
+        def _():
+            to = me - x_at + peer
+            remote(
+                part_out.at[peer], part_in.at[x_at], part_send, part_recv.at[x_at], to, my_summ
+            ).start()
+            remote(
+                stat_out.at[peer], stat_in.at[x_at], stat_send, stat_recv.at[x_at], to, my_summ
+            ).start()
+
+        return carry
+
+    lax.fori_loop(0, X, summary, 0)
+
     to_scalars.wait()
-    first_unit = (me * pow(ROUTER_STRIDE, -1, n_space)) % n_space
     for slot in range(slots):
-        unit = first_unit + slot * n_space
+        unit = me + slot * n_space
 
         @pl.when(unit < 2 * N_UNIT)
         def _():
@@ -434,46 +489,6 @@
                 return carry
 
             lax.fori_loop(0, n_space, pass_on, 0)
-
-    local(values, values, v_recv).wait()
-    for slab in range(YL * CORES):
-        values_t[:, slab * share : (slab + 1) * share] = (
-            values[slab].astype(jnp.float32).T.astype(jnp.bfloat16)
-        )
-    local(keys, keys, k_recv).wait()
-
-    def summary(step, carry):
-        peer = (x_at + step) % X
-
-        @pl.when(step > 0)
-        def _():
-            local(queries.at[peer], queries.at[peer], q_recv.at[peer]).wait()
-
-        theirs = queries[peer]
-        key_rows = keys[...].reshape(YL * CORES * share, LANES)
-        tops, totals, sums = [], [], []
-        for h in range(2):
-            scores = jnp.dot(key_rows, one_head(theirs, h), preferred_element_type=jnp.float32)
-            top, total, summed = attend(scores, values_t[h * HD : (h + 1) * HD, :])
-            tops.append(top)
-            totals.append(total)
-            sums.append(summed)
-        part_out[peer] = jnp.concatenate(sums, axis=0).astype(jnp.bfloat16)
-        stat_out[peer] = jnp.concatenate(tops + totals + [jnp.zeros((4, TOK), jnp.float32)], axis=0)
-
-        @pl.when(step > 0)
-        def _():
-            to = me - x_at + peer
-            remote(
-                part_out.at[peer], part_in.at[x_at], part_send, part_recv.at[x_at], to, my_summ
-            ).start()
-            remote(
-                stat_out.at[peer], stat_in.at[x_at], stat_send, stat_recv.at[x_at], to, my_summ
-            ).start()
-
-        return carry
-
-    lax.fori_loop(0, X, summary, 0)
 
     local(halo, halo, halo_recv).wait()
     halo_k = halo[:N_UNIT].reshape(HALO_KEYS, LANES)
@@ -559,8 +574,8 @@
     for sem, held in ((q_send, queries), (part_send, part_out), (stat_send, stat_out)):
         sent = held.at[: X - 1]
         local(sent, sent, sem).wait()
-    routers = [(unit * ROUTER_STRIDE) % n_space for unit in range(2 * N_UNIT)]
-    own_units = jnp.where(first_unit < (2 * N_UNIT) % n_space, 1, 0) + 2 * N_UNIT // n_space
+    routers = [unit % n_space for unit in range(2 * N_UNIT)]
+    own_units = jnp.where(me < (2 * N_UNIT) % n_space, 1, 0) + 2 * N_UNIT // n_space
     for count in sorted({routers.count(at) for at in range(n_space)}):
 
         @pl.when(own_units == count)
@@ -570,7 +585,7 @@
 
     for slot in range(slots):
 
-        @pl.when(first_unit + slot * n_space < 2 * N_UNIT)
+        @pl.when(me + slot * n_space < 2 * N_UNIT)
         def _():
             sent = staged.at[slot, : n_space - 1]
             local(sent, sent, halo_send).wait()
@@ -605,7 +620,7 @@
         pltpu.VMEM((D, 3 * LANES), bf16),
         pltpu.VMEM((LANES, D), bf16),
         pltpu.VMEM((TOK + HALO_KEYS, TOK), jnp.int32),
-        pltpu.VMEM((SIDE_ROWS, TOK), bf16),
+        pltpu.VMEM((SIDE_ROWS, TOK), f32),
         pltpu.VMEM((2, TOK + HALO_KEYS, TOK), f32),
         pltpu.VMEM(slab, bf16),
         pltpu.VMEM((YL * CORES, share, LANES), bf16),
@@ -656,12 +671,12 @@
         out_specs=vector,
         scratch_shapes=scratch,
         compiler_params=pltpu.CompilerParams(
-            collective_id=0, has_side_effects=True, vmem_limit_bytes=48 * 1024 * 1024
+            collective_id=0, has_side_effects=True, vmem_limit_bytes=63 * 1024 * 1024
         ),
         name="tile_attention",
     )(
         tile_map,
-        pos_bias,
+        pos_bias.transpose(1, 0, 2),
         tokens.reshape(slab),
         norm_gain.reshape(1, D),
         q_weight,
@@ -671,7 +686,7 @@
         sum_keys,
         sum_values,
         jnp.asarray(offset_codes()),
-        jnp.asarray(side_picks(), bf16),
+        jnp.asarray(side_picks()),
     )
     return mixed.reshape(1, BH, BW, LANES)
 

time: 72.3 us -> 60.4 us (0.84)
  local copies, waits for them, and re-layouts: 10.3 us -> 1.47 us
  Pallas kernels: 61.4 us -> 58.8 us
    unnamed x24 -> x1, local copies, waits for them, and re-layouts: 10.3 us -> 1.47 us
    pallas_call x1, Pallas kernels: 61.4 us -> 58.8 us  [shards(): pl.pallas_call(partial(kernel, n_space), out_shape=jax.ShapeDtypeStruct(s...]
where the time goes in v2:
time: 60.4 us; the launch traced here: 60.2 us
  Pallas kernels  58.8 us (97%)
  local copies, waits for them, and re-layouts  1.47 us (2%)
    pallas_call x1, Pallas kernels, shards(): pl.pallas_call(partial(kernel, n_space), out_shape=jax.ShapeDtypeStruct(s...  58.8 us
    unnamed x1, local copies, waits for them, and re-layouts  1.47 us

profile of v2, /device:TPU:1, one launch (start us, length us, event | category | flops | bytes accessed | tf_op | source)
XLA Modules:
  0.0 60.2 jit_solution(8082115866790001508)
XLA Ops:
  0.0 58.8 %tile_attention.1 = bf16[256,128]{1,0:T(8,128)(2,1)} custom-call(s32[64]{0:T(128)} %tile_map.1, f32[7,2,7]{2,1,0:T(2,128)} %bitcast.6, bf16[256,128]{1,0:T(8,128)(2,1)} %bitcast.5, f32[1,1024]{1,0:T(1,128)} %bitcast.7, bf16[1024,128]{1,0:T(8,128)(2,1)} %q_weight.1, bf16[1024,128]{1,0:T(8,128)(2,1)} %k_weight.1, bf16[1024,128]{1,0:T(8,128)(2,1)} %v_weight.1, ...), custom_call_target="tpu_custom_call" | custom-call | tf_op jit(solution)/shard_map/tile_attention/pallas_call | solution.py:667
  58.8 1.5 %copy.14 = bf16[1,8,32,128]{3,2,1,0:T(8,128)(2,1)} copy(bf16[1,8,32,128]{3,2,1,0:T(8,128)(2,1)} %bitcast.4) | data formatting | bytes 131072

commit v3 on v2

--- a/solution.py
+++ b/solution.py
@@ -35,7 +35,7 @@
 HALO_KEYS = N_UNIT * UNIT
 BAND = HALO * BW
 SIDE_ROWS = HALO_KEYS - 2 * BAND
-LATE_Z = 5
+LATE_Z = 4
 MESH = pl.DeviceIdType.MESH
 
 
@@ -124,6 +124,7 @@
     line_in,
     load_sem,
     inverse_sem,
+    entered,
     tok_send,
     tok_recv,
     k_send,
@@ -146,7 +147,7 @@
     line_recv,
 ):
     slots = routed.shape[0]
-    n_routers = min(n_space, 2 * N_UNIT)
+    hub = n_space - 1
     share = keys.shape[1]
     ty = n_space // TX
     me = lax.axis_index("space")
@@ -178,21 +179,6 @@
     def line(step):
         return (y_lo + step) % YL
 
-    loads = [
-        local(q_weight, weights.at[:, 0:LANES], load_sem.at[0]),
-        local(k_weight, weights.at[:, LANES : 2 * LANES], load_sem.at[1]),
-        local(v_weight, weights.at[:, 2 * LANES : 3 * LANES], load_sem.at[2]),
-        local(out_weight, out_w, load_sem.at[3]),
-        local(codes_in, codes, load_sem.at[4]),
-        local(picks_in, picks, load_sem.at[5]),
-    ]
-    own_tokens = local(tokens, gathered.at[my_summ], tok_recv.at[my_summ])
-    own_tokens.start()
-    my_rows = pl.ds(pl.multiple_of(x_at * share, share), share)
-    my_cols = pl.ds(pl.multiple_of(my_summ * LANES, LANES), LANES)
-    local(sum_keys.at[my_rows, my_cols], keys.at[my_summ], k_recv).start()
-    local(sum_values.at[my_rows, my_cols], values.at[my_summ], v_recv).start()
-
     barrier = pltpu.get_barrier_semaphore()
 
     def greet(space, summ):
@@ -208,18 +194,91 @@
     for step in range(1, X):
         greet(me - x_at + (x_at + step) % X, my_summ)
 
-    def greet_space(step, carry):
-        greet((me + step) % n_space, my_summ)
-        return carry
-
-    @pl.when(me < n_routers)
-    def _():
-        lax.fori_loop(1, n_space, greet_space, 0)
-
+    @pl.when(me != hub)
+    def _():
+        greet(hub, my_summ)
+
+    loads = [
+        local(codes_in, codes, load_sem.at[0]),
+        local(k_weight, weights.at[:, LANES : 2 * LANES], load_sem.at[1]),
+        local(v_weight, weights.at[:, 2 * LANES : 3 * LANES], load_sem.at[2]),
+        local(q_weight, weights.at[:, 0:LANES], load_sem.at[3]),
+        local(picks_in, picks, load_sem.at[4]),
+        local(out_weight, out_w, load_sem.at[5]),
+    ]
+    own_tokens = local(tokens, gathered.at[my_summ], tok_recv.at[my_summ])
+    own_tokens.start()
     for load in loads:
         load.start()
+    my_rows = pl.ds(pl.multiple_of(x_at * share, share), share)
+    my_cols = pl.ds(pl.multiple_of(my_summ * LANES, LANES), LANES)
+    local(sum_keys.at[my_rows, my_cols], keys.at[my_summ], k_recv).start()
+    local(sum_values.at[my_rows, my_cols], values.at[my_summ], v_recv).start()
+
+    to_scalars = local(inverse, inverse_s, inverse_sem)
+
+    def prepare():
+        lane = lax.broadcasted_iota(jnp.int32, inverse.shape, 1)
+
+        def place(at, so_far):
+            return so_far + jnp.where(lane == tile_map[at], at, 0)
+
+        inverse[...] = lax.fori_loop(0, n_space, place, jnp.zeros(inverse.shape, jnp.int32))
+        to_scalars.start()
+
+        loads[0].wait()
+
+        def fill(at, carry):
+            rows = pl.ds(pl.multiple_of(at * UNIT, UNIT), UNIT)
+            code = codes[rows, :]
+            first = jnp.full(code.shape, HIDDEN, jnp.float32)
+            second = first
+            for i in range(WIN):
+                for j in range(WIN):
+                    here = code == i * WIN + j
+                    first = jnp.where(here, pos_bias[i, 0, j], first)
+                    second = jnp.where(here, pos_bias[i, 1, j], second)
+            bias[0, rows, :] = first
+            bias[1, rows, :] = second
+            return carry
+
+        lax.fori_loop(0, bias.shape[1] // UNIT, fill, 0)
+        my_tile = tile_map[me]
+        tile_row, tile_col = my_tile // TX, my_tile % TX
+        edge = {
+            (-1, 0): jnp.where(tile_row > 0, 0.0, HIDDEN),
+            (1, 0): jnp.where(tile_row < ty - 1, 0.0, HIDDEN),
+            (0, -1): jnp.where(tile_col > 0, 0.0, HIDDEN),
+            (0, 1): jnp.where(tile_col < TX - 1, 0.0, HIDDEN),
+        }
+        for down in (-1, 1):
+            for across in (-1, 1):
+                edge[down, across] = jnp.minimum(edge[down, 0], edge[0, across])
+        for step, hidden in edge.items():
+            at = TOK + UNIT_STEP.index(step) * UNIT
+            rows = slice(at, at + UNIT_STEP.count(step) * UNIT)
+            for h in range(2):
+                bias[h, rows, :] = bias[h, rows, :] + hidden
+
+    @pl.when(z_at < LATE_Z)
+    def _():
+        prepare()
+
     near = 1 + (YL - 1) + 4 * CORES + (X - 1)
-    pl.semaphore_wait(barrier, near + n_routers - jnp.where(me < n_routers, 1, 0))
+    pl.semaphore_wait(barrier, near + jnp.where(me == hub, n_space - 1, 0))
+
+    @pl.when(me == hub)
+    def _():
+        def tell(step, carry):
+            pl.semaphore_signal(
+                entered,
+                inc=1,
+                device_id=((me + step) % n_space, my_summ),
+                device_id_type=MESH,
+            )
+            return carry
+
+        lax.fori_loop(1, n_space, tell, 0)
 
     sends = []
     for at, step in enumerate((2, 1, 3)):
@@ -260,49 +319,6 @@
     @pl.when(z_at < LATE_Z)
     def _():
         give_summary()
-
-    lane = lax.broadcasted_iota(jnp.int32, inverse.shape, 1)
-
-    def place(at, so_far):
-        return so_far + jnp.where(lane == tile_map[at], at, 0)
-
-    inverse[...] = lax.fori_loop(0, n_space, place, jnp.zeros(inverse.shape, jnp.int32))
-    to_scalars = local(inverse, inverse_s, inverse_sem)
-    to_scalars.start()
-
-    loads[4].wait()
-
-    def fill(at, carry):
-        rows = pl.ds(pl.multiple_of(at * UNIT, UNIT), UNIT)
-        code = codes[rows, :]
-        first = jnp.full(code.shape, HIDDEN, jnp.float32)
-        second = first
-        for i in range(WIN):
-            for j in range(WIN):
-                here = code == i * WIN + j
-                first = jnp.where(here, pos_bias[i, 0, j], first)
-                second = jnp.where(here, pos_bias[i, 1, j], second)
-        bias[0, rows, :] = first
-        bias[1, rows, :] = second
-        return carry
-
-    lax.fori_loop(0, bias.shape[1] // UNIT, fill, 0)
-    my_tile = tile_map[me]
-    tile_row, tile_col = my_tile // TX, my_tile % TX
-    edge = {
-        (-1, 0): jnp.where(tile_row > 0, 0.0, HIDDEN),
-        (1, 0): jnp.where(tile_row < ty - 1, 0.0, HIDDEN),
-        (0, -1): jnp.where(tile_col > 0, 0.0, HIDDEN),
-        (0, 1): jnp.where(tile_col < TX - 1, 0.0, HIDDEN),
-    }
-    for down in (-1, 1):
-        for across in (-1, 1):
-            edge[down, across] = jnp.minimum(edge[down, 0], edge[0, across])
-    for step, hidden in edge.items():
-        at = TOK + UNIT_STEP.index(step) * UNIT
-        rows = slice(at, at + UNIT_STEP.count(step) * UNIT)
-        for h in range(2):
-            bias[h, rows, :] = bias[h, rows, :] + hidden
 
     forwards = []
     for at, step in enumerate((1, 3, 2)):
@@ -332,14 +348,14 @@
         cols = slice(slab * LANES, (slab + 1) * LANES)
         floats = gathered[slab].astype(jnp.float32)
         normed[:, cols] = (floats * scale * gain[:, cols]).astype(jnp.bfloat16)
-    for load in loads[:3]:
+    for load in loads[1:3]:
         load.wait()
     own_kv = jnp.dot(normed[...], weights[:, LANES:], preferred_element_type=jnp.float32)
     own_kv = own_kv.astype(jnp.bfloat16)
     own_k[...] = own_kv[:, :LANES]
     own_v = own_kv[:, LANES:]
 
-    loads[5].wait()
+    loads[4].wait()
     sides = jnp.dot(picks[...].astype(jnp.bfloat16), own_kv, preferred_element_type=jnp.float32)
     sides = sides.astype(jnp.bfloat16)
     for which in range(2):
@@ -373,8 +389,13 @@
 
         return carry
 
+    @pl.when(me != hub)
+    def _():
+        pl.semaphore_wait(entered, 1)
+
     lax.fori_loop(0, 2 * N_UNIT, send_rim, 0)
 
+    loads[3].wait()
     own_q = jnp.dot(normed[...], weights[:, :LANES], preferred_element_type=jnp.float32)
     scaled = own_q.astype(jnp.bfloat16).astype(jnp.float32) * HD ** (-0.5)
     queries[x_at] = scaled.T.astype(jnp.bfloat16)
@@ -401,12 +422,60 @@
         summed = jnp.dot(v_rows, weight.astype(jnp.bfloat16), preferred_element_type=jnp.float32)
         return top, total, summed
 
+    @pl.when(z_at >= LATE_Z)
+    def _():
+        prepare()
+
     my_queries = queries[x_at]
     own_vt = own_v.astype(jnp.float32).T.astype(jnp.bfloat16)
     parts = [[], []]
     for h in range(2):
         scores = jnp.dot(own_k[...], one_head(my_queries, h), preferred_element_type=jnp.float32)
         parts[h].append(attend(scores + bias[h, :TOK], own_vt[h * HD : (h + 1) * HD]))
+
+    to_scalars.wait()
+
+    def route():
+        for slot in range(slots):
+            unit = me + slot * n_space
+
+            @pl.when(unit < 2 * N_UNIT)
+            def _():
+                local(routed.at[slot], routed.at[slot], rim_recv.at[slot]).wait()
+                kind = unit % N_UNIT
+                down = jnp.where(
+                    kind < 6, -1, jnp.where(kind < 12, 1, jnp.where(kind < 16, 0, jnp.where(kind < 18, -1, 1)))
+                )
+                across = jnp.where(
+                    kind < 12,
+                    0,
+                    jnp.where(kind < 14, -1, jnp.where(kind < 16, 1, jnp.where(kind % 2 == 0, -1, 1))),
+                )
+
+                def pass_on(to, carry):
+                    tile = tile_map[to]
+                    row = jnp.clip(tile // TX + down, 0, ty - 1)
+                    col = jnp.clip(tile % TX + across, 0, TX - 1)
+                    holder = jnp.clip(inverse_s[0, row * TX + col], 0, n_space - 1)
+                    staged[slot, to] = routed[slot, holder]
+
+                    @pl.when(to != me)
+                    def _():
+                        remote(
+                            staged.at[slot, to], halo.at[unit], halo_send, halo_recv, to, my_summ
+                        ).start()
+
+                    @pl.when(to == me)
+                    def _():
+                        local(staged.at[slot, to], halo.at[unit], halo_recv).start()
+
+                    return carry
+
+                lax.fori_loop(0, n_space, pass_on, 0)
+
+    @pl.when(z_at >= LATE_Z)
+    def _():
+        route()
 
     @pl.when(z_at >= LATE_Z)
     def _():
@@ -452,43 +521,9 @@
 
     lax.fori_loop(0, X, summary, 0)
 
-    to_scalars.wait()
-    for slot in range(slots):
-        unit = me + slot * n_space
-
-        @pl.when(unit < 2 * N_UNIT)
-        def _():
-            local(routed.at[slot], routed.at[slot], rim_recv.at[slot]).wait()
-            kind = unit % N_UNIT
-            down = jnp.where(
-                kind < 6, -1, jnp.where(kind < 12, 1, jnp.where(kind < 16, 0, jnp.where(kind < 18, -1, 1)))
-            )
-            across = jnp.where(
-                kind < 12,
-                0,
-                jnp.where(kind < 14, -1, jnp.where(kind < 16, 1, jnp.where(kind % 2 == 0, -1, 1))),
-            )
-
-            def pass_on(to, carry):
-                tile = tile_map[to]
-                row = jnp.clip(tile // TX + down, 0, ty - 1)
-                col = jnp.clip(tile % TX + across, 0, TX - 1)
-                holder = jnp.clip(inverse_s[0, row * TX + col], 0, n_space - 1)
-                staged[slot, to] = routed[slot, holder]
-
-                @pl.when(to != me)
-                def _():
-                    remote(
-                        staged.at[slot, to], halo.at[unit], halo_send, halo_recv, to, my_summ
-                    ).start()
-
-                @pl.when(to == me)
-                def _():
-                    local(staged.at[slot, to], halo.at[unit], halo_recv).start()
-
-                return carry
-
-            lax.fori_loop(0, n_space, pass_on, 0)
+    @pl.when(z_at < LATE_Z)
+    def _():
+        route()
 
     local(halo, halo, halo_recv).wait()
     halo_k = halo[:N_UNIT].reshape(HALO_KEYS, LANES)
@@ -527,7 +562,7 @@
         heads.append(summed / total)
     attended = jnp.concatenate(heads, axis=0).T.astype(jnp.bfloat16)
 
-    loads[3].wait()
+    loads[5].wait()
     mixed = jnp.dot(attended, out_w[...], preferred_element_type=jnp.float32).astype(jnp.bfloat16)
     for at in range(YL):
         for side in range(CORES):
@@ -643,6 +678,7 @@
         pltpu.VMEM((YL,) + slab, bf16),
         dma((6,)),
         dma,
+        pltpu.SemaphoreType.REGULAR,
         dma((7,)),
         dma((YL * CORES,)),
         dma,

time: 60.4 us -> 62.4 us (1.033)
  the two profiles are of different devices: /device:TPU:1 before, /device:TPU:267 now
where the time goes in v3:
time: 62.4 us; the launch traced here: 62.2 us
  Pallas kernels  60.7 us (97%)
  local copies, waits for them, and re-layouts  1.47 us (2%)
    pallas_call x1, Pallas kernels, shards(): pl.pallas_call(partial(kernel, n_space), out_shape=jax.ShapeDtypeStruct(s...  60.7 us
    unnamed x1, local copies, waits for them, and re-layouts  1.47 us

profile of v3, /device:TPU:267, one launch (start us, length us, event | category | flops | bytes accessed | tf_op | source)
XLA Modules:
  0.0 62.2 jit_solution(17719270913001922929)
XLA Ops:
  0.0 60.7 %tile_attention.1 = bf16[256,128]{1,0:T(8,128)(2,1)} custom-call(s32[64]{0:T(128)} %tile_map.1, f32[7,2,7]{2,1,0:T(2,128)} %bitcast.6, bf16[256,128]{1,0:T(8,128)(2,1)} %bitcast.5, f32[1,1024]{1,0:T(1,128)} %bitcast.7, bf16[1024,128]{1,0:T(8,128)(2,1)} %q_weight.1, bf16[1024,128]{1,0:T(8,128)(2,1)} %k_weight.1, bf16[1024,128]{1,0:T(8,128)(2,1)} %v_weight.1, ...), custom_call_target="tpu_custom_call" | custom-call | tf_op jit(solution)/shard_map/tile_attention/pallas_call | solution.py:703
  60.7 1.5 %copy.14 = bf16[1,8,32,128]{3,2,1,0:T(8,128)(2,1)} copy(bf16[1,8,32,128]{3,2,1,0:T(8,128)(2,1)} %bitcast.4) | data formatting | bytes 131072

commit v4 on v3

--- a/solution.py
+++ b/solution.py
@@ -35,7 +35,7 @@
 HALO_KEYS = N_UNIT * UNIT
 BAND = HALO * BW
 SIDE_ROWS = HALO_KEYS - 2 * BAND
-LATE_Z = 4
+LATE_Z = 5
 MESH = pl.DeviceIdType.MESH
 
 
@@ -475,10 +475,6 @@
 
     @pl.when(z_at >= LATE_Z)
     def _():
-        route()
-
-    @pl.when(z_at >= LATE_Z)
-    def _():
         give_summary()
 
     local(values, values, v_recv).wait()
@@ -519,11 +515,10 @@
 
         return carry
 
-    lax.fori_loop(0, X, summary, 0)
-
-    @pl.when(z_at < LATE_Z)
-    def _():
-        route()
+    before = jnp.clip(X - (z_at + 1) // 2 - 2 * y_hi, 0, X)
+    lax.fori_loop(0, before, summary, 0)
+    route()
+    lax.fori_loop(before, X, summary, 0)
 
     local(halo, halo, halo_recv).wait()
     halo_k = halo[:N_UNIT].reshape(HALO_KEYS, LANES)

time: 62.4 us -> 55.8 us (0.89)
  the two profiles are of different devices: /device:TPU:267 before, /device:TPU:1 now
where the time goes in v4:
time: 55.8 us; the launch traced here: 55.6 us
  Pallas kernels  54.1 us (97%)
  local copies, waits for them, and re-layouts  1.47 us (3%)
    pallas_call x1, Pallas kernels, shards(): pl.pallas_call(partial(kernel, n_space), out_shape=jax.ShapeDtypeStruct(s...  54.1 us
    unnamed x1, local copies, waits for them, and re-layouts  1.47 us

profile of v4, /device:TPU:1, one launch (start us, length us, event | category | flops | bytes accessed | tf_op | source)
XLA Modules:
  0.0 55.6 jit_solution(5439879134794437961)
XLA Ops:
  0.0 54.1 %tile_attention.1 = bf16[256,128]{1,0:T(8,128)(2,1)} custom-call(s32[64]{0:T(128)} %tile_map.1, f32[7,2,7]{2,1,0:T(2,128)} %bitcast.6, bf16[256,128]{1,0:T(8,128)(2,1)} %bitcast.5, f32[1,1024]{1,0:T(1,128)} %bitcast.7, bf16[1024,128]{1,0:T(8,128)(2,1)} %q_weight.1, bf16[1024,128]{1,0:T(8,128)(2,1)} %k_weight.1, bf16[1024,128]{1,0:T(8,128)(2,1)} %v_weight.1, ...), custom_call_target="tpu_custom_call" | custom-call | tf_op jit(solution)/shard_map/tile_attention/pallas_call | solution.py:698
  54.1 1.5 %copy.14 = bf16[1,8,32,128]{3,2,1,0:T(8,128)(2,1)} copy(bf16[1,8,32,128]{3,2,1,0:T(8,128)(2,1)} %bitcast.4) | data formatting | bytes 131072

commit v5 on v4

--- a/solution.py
+++ b/solution.py
@@ -83,10 +83,10 @@
 
 def kernel(
     n_space,
-    tile_map,
-    pos_bias,
+    tile_map_in,
+    pos_bias_in,
     tokens,
-    gain,
+    gain_in,
     q_weight,
     k_weight,
     v_weight,
@@ -96,6 +96,9 @@
     codes_in,
     picks_in,
     out,
+    tile_map,
+    pos_bias,
+    gain,
     gathered,
     normed,
     weights,
@@ -103,7 +106,7 @@
     codes,
     picks,
     bias,
-    own_k,
+    own_kv,
     keys,
     values,
     values_t,
@@ -205,9 +208,17 @@
         local(q_weight, weights.at[:, 0:LANES], load_sem.at[3]),
         local(picks_in, picks, load_sem.at[4]),
         local(out_weight, out_w, load_sem.at[5]),
+        local(gain_in, gain, load_sem.at[6]),
+        local(tile_map_in, tile_map, load_sem.at[7]),
+        local(pos_bias_in, pos_bias, load_sem.at[8]),
     ]
-    own_tokens = local(tokens, gathered.at[my_summ], tok_recv.at[my_summ])
-    own_tokens.start()
+    half_rows = [pl.ds(half * (TOK // 2), TOK // 2) for half in range(2)]
+    own_tokens = [
+        local(tokens.at[rows], gathered.at[my_summ, rows], tok_recv.at[half, my_summ])
+        for half, rows in enumerate(half_rows)
+    ]
+    for load in own_tokens:
+        load.start()
     for load in loads:
         load.start()
     my_rows = pl.ds(pl.multiple_of(x_at * share, share), share)
@@ -218,6 +229,7 @@
     to_scalars = local(inverse, inverse_s, inverse_sem)
 
     def prepare():
+        loads[7].wait()
         lane = lax.broadcasted_iota(jnp.int32, inverse.shape, 1)
 
         def place(at, so_far):
@@ -227,6 +239,7 @@
         to_scalars.start()
 
         loads[0].wait()
+        loads[8].wait()
 
         def fill(at, carry):
             rows = pl.ds(pl.multiple_of(at * UNIT, UNIT), UNIT)
@@ -281,22 +294,20 @@
         lax.fori_loop(1, n_space, tell, 0)
 
     sends = []
-    for at, step in enumerate((2, 1, 3)):
+
+    def send_slab(source, slab, half, summ):
+        at = gathered.at[slab, half_rows[half]]
         sends.append(
             remote(
-                tokens,
-                gathered.at[my_summ],
-                tok_send.at[at],
-                tok_recv.at[my_summ],
-                me,
-                line(step) * CORES + core,
+                source, at, tok_send.at[len(sends)], tok_recv.at[half, slab], me, summ
             )
         )
-    sends.append(
-        remote(tokens, gathered.at[my_summ], tok_send.at[3], tok_recv.at[my_summ], me, sibling)
-    )
-    for send in sends:
-        send.start()
+        sends[-1].start()
+
+    for half in range(2):
+        for step in (2, 1, 3):
+            send_slab(tokens.at[half_rows[half]], my_summ, half, line(step) * CORES + core)
+        send_slab(tokens.at[half_rows[half]], my_summ, half, sibling)
 
     def give(source, held, send_sem, recv_sem, space, summ):
         cols = pl.ds(pl.multiple_of(summ * LANES, LANES), LANES)
@@ -320,53 +331,34 @@
     def _():
         give_summary()
 
-    forwards = []
-    for at, step in enumerate((1, 3, 2)):
-        slab = line(step) * CORES + core
-        local(gathered.at[slab], gathered.at[slab], tok_recv.at[slab]).wait()
-        forward = remote(
-            gathered.at[slab],
-            gathered.at[slab],
-            tok_send.at[4 + at],
-            tok_recv.at[slab],
-            me,
-            sibling,
-        )
-        forward.start()
-        forwards.append(forward)
-    own_tokens.wait()
-    for step in range(YL):
-        slab = line(step) * CORES + 1 - core
-        local(gathered.at[slab], gathered.at[slab], tok_recv.at[slab]).wait()
-
-    squares = jnp.zeros((TOK, LANES), jnp.float32)
-    for slab in range(YL * CORES):
-        floats = gathered[slab].astype(jnp.float32)
-        squares = squares + floats * floats
-    scale = lax.rsqrt(jnp.sum(squares, axis=-1, keepdims=True) * (1.0 / D) + EPSILON)
-    for slab in range(YL * CORES):
-        cols = slice(slab * LANES, (slab + 1) * LANES)
-        floats = gathered[slab].astype(jnp.float32)
-        normed[:, cols] = (floats * scale * gain[:, cols]).astype(jnp.bfloat16)
-    for load in loads[1:3]:
-        load.wait()
-    own_kv = jnp.dot(normed[...], weights[:, LANES:], preferred_element_type=jnp.float32)
-    own_kv = own_kv.astype(jnp.bfloat16)
-    own_k[...] = own_kv[:, :LANES]
-    own_v = own_kv[:, LANES:]
-
-    loads[4].wait()
-    sides = jnp.dot(picks[...].astype(jnp.bfloat16), own_kv, preferred_element_type=jnp.float32)
-    sides = sides.astype(jnp.bfloat16)
-    for which in range(2):
-        own = own_kv[:, which * LANES : (which + 1) * LANES]
-        first = which * N_UNIT
-        bands = BAND // UNIT
-        pack[first : first + bands] = own[TOK - BAND :].reshape(bands, UNIT, LANES)
-        pack[first + bands : first + 2 * bands] = own[:BAND].reshape(bands, UNIT, LANES)
-        pack[first + 2 * bands : first + N_UNIT] = sides[
-            :, which * LANES : (which + 1) * LANES
-        ].reshape(N_UNIT - 2 * bands, UNIT, LANES)
+    def await_slab(slab, half):
+        held = gathered.at[slab, half_rows[half]]
+        local(held, held, tok_recv.at[half, slab]).wait()
+
+    def await_half(half):
+        for step in (1, 3, 2):
+            slab = line(step) * CORES + core
+            await_slab(slab, half)
+            send_slab(gathered.at[slab, half_rows[half]], slab, half, sibling)
+        own_tokens[half].wait()
+        for step in range(YL):
+            await_slab(line(step) * CORES + 1 - core, half)
+
+    def project_half(half):
+        rows = half_rows[half]
+        squares = jnp.zeros((TOK // 2, LANES), jnp.float32)
+        for slab in range(YL * CORES):
+            floats = gathered[slab, rows, :].astype(jnp.float32)
+            squares = squares + floats * floats
+        scale = lax.rsqrt(jnp.sum(squares, axis=-1, keepdims=True) * (1.0 / D) + EPSILON)
+        for slab in range(YL * CORES):
+            cols = slice(slab * LANES, (slab + 1) * LANES)
+            floats = gathered[slab, rows, :].astype(jnp.float32)
+            normed[rows, cols] = (floats * scale * gain[:, cols]).astype(jnp.bfloat16)
+        result = jnp.dot(normed[rows, :], weights[:, LANES:], preferred_element_type=jnp.float32)
+        own_kv[rows, :] = result.astype(jnp.bfloat16)
+
+    bands = BAND // UNIT
 
     def send_rim(unit, carry):
         router = unit % n_space
@@ -389,17 +381,68 @@
 
         return carry
 
+    await_half(0)
+    loads[6].wait()
+    for load in loads[1:3]:
+        load.wait()
+    project_half(0)
+
     @pl.when(me != hub)
     def _():
         pl.semaphore_wait(entered, 1)
 
-    lax.fori_loop(0, 2 * N_UNIT, send_rim, 0)
+    for which in range(2):
+        cols = slice(which * LANES, (which + 1) * LANES)
+        first = which * N_UNIT + bands
+        pack[first : first + bands] = own_kv[:BAND, cols].reshape(bands, UNIT, LANES)
+        lax.fori_loop(first, first + bands, send_rim, 0)
+    await_half(1)
+    project_half(1)
+    loads[4].wait()
+    sides = jnp.dot(
+        picks[...].astype(jnp.bfloat16), own_kv[...], preferred_element_type=jnp.float32
+    )
+    sides = sides.astype(jnp.bfloat16)
+    for which in range(2):
+        cols = slice(which * LANES, (which + 1) * LANES)
+        first = which * N_UNIT
+        pack[first : first + bands] = own_kv[TOK - BAND :, cols].reshape(bands, UNIT, LANES)
+        pack[first + 2 * bands : first + N_UNIT] = sides[:, cols].reshape(
+            N_UNIT - 2 * bands, UNIT, LANES
+        )
+        lax.fori_loop(first, first + bands, send_rim, 0)
+        lax.fori_loop(first + 2 * bands, first + N_UNIT, send_rim, 0)
+    own_k = own_kv[:, :LANES]
+    own_v = own_kv[:, LANES:]
 
     loads[3].wait()
     own_q = jnp.dot(normed[...], weights[:, :LANES], preferred_element_type=jnp.float32)
     scaled = own_q.astype(jnp.bfloat16).astype(jnp.float32) * HD ** (-0.5)
     queries[x_at] = scaled.T.astype(jnp.bfloat16)
     peers = [(x_at + step) % X for step in range(X)]
+    def one_head(both, h):
+        blank = jnp.zeros((HD, TOK), jnp.bfloat16)
+        own = both[h * HD : (h + 1) * HD]
+        return jnp.concatenate([own, blank] if h == 0 else [blank, own], axis=0)
+
+    def attend(scores, v_rows):
+        top = jnp.max(scores, axis=0, keepdims=True)
+        weight = jnp.exp(scores - top)
+        total = jnp.sum(weight, axis=0, keepdims=True)
+        summed = jnp.dot(v_rows, weight.astype(jnp.bfloat16), preferred_element_type=jnp.float32)
+        return top, total, summed
+
+    @pl.when(z_at >= LATE_Z)
+    def _():
+        prepare()
+
+    my_queries = queries[x_at]
+    own_vt = own_v.astype(jnp.float32).T.astype(jnp.bfloat16)
+    parts = [[], []]
+    for h in range(2):
+        scores = jnp.dot(own_k, one_head(my_queries, h), preferred_element_type=jnp.float32)
+        parts[h].append(attend(scores + bias[h, :TOK], own_vt[h * HD : (h + 1) * HD]))
+
     for step in range(1, X):
         remote(
             queries.at[x_at],
@@ -409,29 +452,6 @@
             me - x_at + peers[step],
             my_summ,
         ).start()
-
-    def one_head(both, h):
-        blank = jnp.zeros((HD, TOK), jnp.bfloat16)
-        own = both[h * HD : (h + 1) * HD]
-        return jnp.concatenate([own, blank] if h == 0 else [blank, own], axis=0)
-
-    def attend(scores, v_rows):
-        top = jnp.max(scores, axis=0, keepdims=True)
-        weight = jnp.exp(scores - top)
-        total = jnp.sum(weight, axis=0, keepdims=True)
-        summed = jnp.dot(v_rows, weight.astype(jnp.bfloat16), preferred_element_type=jnp.float32)
-        return top, total, summed
-
-    @pl.when(z_at >= LATE_Z)
-    def _():
-        prepare()
-
-    my_queries = queries[x_at]
-    own_vt = own_v.astype(jnp.float32).T.astype(jnp.bfloat16)
-    parts = [[], []]
-    for h in range(2):
-        scores = jnp.dot(own_k[...], one_head(my_queries, h), preferred_element_type=jnp.float32)
-        parts[h].append(attend(scores + bias[h, :TOK], own_vt[h * HD : (h + 1) * HD]))
 
     to_scalars.wait()
 
@@ -452,7 +472,8 @@
                     jnp.where(kind < 14, -1, jnp.where(kind < 16, 1, jnp.where(kind % 2 == 0, -1, 1))),
                 )
 
-                def pass_on(to, carry):
+                def pass_on(at, carry):
+                    to = at // 8 * 8 + (at + me) % 8
                     tile = tile_map[to]
                     row = jnp.clip(tile // TX + down, 0, ty - 1)
                     col = jnp.clip(tile % TX + across, 0, TX - 1)
@@ -476,6 +497,12 @@
     @pl.when(z_at >= LATE_Z)
     def _():
         give_summary()
+
+    before = jnp.where(y_hi == 0, jnp.clip(X - z_at, 0, X), jnp.where(z_at == 0, 2, 0))
+
+    @pl.when(before == 0)
+    def _():
+        route()
 
     local(values, values, v_recv).wait()
     for slab in range(YL * CORES):
@@ -515,9 +542,12 @@
 
         return carry
 
-    before = jnp.clip(X - (z_at + 1) // 2 - 2 * y_hi, 0, X)
     lax.fori_loop(0, before, summary, 0)
-    route()
+
+    @pl.when(before > 0)
+    def _():
+        route()
+
     lax.fori_loop(before, X, summary, 0)
 
     local(halo, halo, halo_recv).wait()
@@ -596,7 +626,7 @@
         result = result + line_in[at].astype(jnp.float32)
     out[...] = result.astype(jnp.bfloat16)
 
-    for send in sends + forwards + pair + along:
+    for send in sends + pair + along:
         send.wait_send()
     for sem, held in ((k_send, keys), (v_send, values)):
         sent = held.at[: YL * CORES - 1]
@@ -640,11 +670,13 @@
     f32 = jnp.float32
     dma = pltpu.SemaphoreType.DMA
     anywhere = pl.BlockSpec(memory_space=pl.ANY)
-    scalars = pl.BlockSpec(memory_space=pltpu.SMEM)
     vector = pl.BlockSpec(memory_space=pltpu.VMEM)
     slab = (TOK, LANES)
     turned = (LANES, TOK)
     scratch = [
+        pltpu.SMEM((n_space,), jnp.int32),
+        pltpu.SMEM((WIN, 2, WIN), f32),
+        pltpu.VMEM((1, D), f32),
         pltpu.VMEM((YL * CORES,) + slab, bf16),
         pltpu.VMEM((TOK, D), bf16),
         pltpu.VMEM((D, 3 * LANES), bf16),
@@ -652,7 +684,7 @@
         pltpu.VMEM((TOK + HALO_KEYS, TOK), jnp.int32),
         pltpu.VMEM((SIDE_ROWS, TOK), f32),
         pltpu.VMEM((2, TOK + HALO_KEYS, TOK), f32),
-        pltpu.VMEM(slab, bf16),
+        pltpu.VMEM((TOK, 2 * LANES), bf16),
         pltpu.VMEM((YL * CORES, share, LANES), bf16),
         pltpu.VMEM((YL * CORES, share, LANES), bf16),
         pltpu.VMEM((LANES, YL * CORES * share), bf16),
@@ -671,11 +703,11 @@
         pltpu.VMEM((YL,) + slab, bf16),
         pltpu.VMEM((YL,) + slab, bf16),
         pltpu.VMEM((YL,) + slab, bf16),
-        dma((6,)),
+        dma((9,)),
         dma,
         pltpu.SemaphoreType.REGULAR,
-        dma((7,)),
-        dma((YL * CORES,)),
+        dma((14,)),
+        dma((2, YL * CORES)),
         dma,
         dma,
         dma,
@@ -698,7 +730,7 @@
     mixed = pl.pallas_call(
         partial(kernel, n_space),
         out_shape=jax.ShapeDtypeStruct(slab, bf16),
-        in_specs=[scalars, scalars, anywhere, vector] + [anywhere] * 8,
+        in_specs=[anywhere] * 12,
         out_specs=vector,
         scratch_shapes=scratch,
         compiler_params=pltpu.CompilerParams(

time: 55.8 us -> 54 us (0.968)
  Pallas kernels: 54.1 us -> 52.4 us
    pallas_call x1, Pallas kernels: 54.1 us -> 52.4 us  [shards(): pl.pallas_call(partial(kernel, n_space), out_shape=jax.ShapeDtypeStruct(s...]
where the time goes in v5:
time: 54 us; the launch traced here: 53.9 us
  Pallas kernels  52.4 us (97%)
  local copies, waits for them, and re-layouts  1.47 us (3%)
    pallas_call x1, Pallas kernels, shards(): pl.pallas_call(partial(kernel, n_space), out_shape=jax.ShapeDtypeStruct(s...  52.4 us
    unnamed x1, local copies, waits for them, and re-layouts  1.47 us

profile of v5, /device:TPU:1, one launch (start us, length us, event | category | flops | bytes accessed | tf_op | source)
XLA Modules:
  0.0 53.9 jit_solution(9237252809187387123)
XLA Ops:
  0.0 52.4 %tile_attention.1 = bf16[256,128]{1,0:T(8,128)(2,1)} custom-call(s32[64]{0:T(128)} %tile_map_in.1, f32[7,2,7]{2,1,0:T(2,128)} %bitcast.6, bf16[256,128]{1,0:T(8,128)(2,1)} %bitcast.5, f32[1,1024]{1,0:T(1,128)} %bitcast.7, bf16[1024,128]{1,0:T(8,128)(2,1)} %q_weight.1, bf16[1024,128]{1,0:T(8,128)(2,1)} %k_weight.1, bf16[1024,128]{1,0:T(8,128)(2,1)} %v_weight.1, ...), custom_call_target="tpu_custom_call" | custom-call | tf_op jit(solution)/shard_map/tile_attention/pallas_call | solution.py:730
  52.4 1.5 %copy.14 = bf16[1,8,32,128]{3,2,1,0:T(8,128)(2,1)} copy(bf16[1,8,32,128]{3,2,1,0:T(8,128)(2,1)} %bitcast.4) | data formatting | bytes 131072

commit v6 on v5

--- a/solution.py
+++ b/solution.py
@@ -593,7 +593,9 @@
         for side in range(CORES):
             slab = at * CORES + side
             terms[side, at] = mixed[:, slab * LANES : (slab + 1) * LANES]
-    order = [line(step) for step in (2, 1, 3, 0)]
+    rank = jnp.where(y_hi == 0, y_lo, YL - 1 - y_lo)
+    others = [at + jnp.where(rank <= at, 1, 0) for at in range(YL - 1)]
+    order = [jnp.where(y_hi == 0, other, YL - 1 - other) for other in others] + [y_lo]
     pair = []
     for at in order:
         pair.append(

time: 54 us -> 54.1 us (level)
  no operation moved by 1% of the time
where the time goes in v6:
time: 54.1 us; the launch traced here: 53.9 us
  Pallas kernels  52.4 us (97%)
  local copies, waits for them, and re-layouts  1.47 us (3%)
    pallas_call x1, Pallas kernels, shards(): pl.pallas_call(partial(kernel, n_space), out_shape=jax.ShapeDtypeStruct(s...  52.4 us
    unnamed x1, local copies, waits for them, and re-layouts  1.47 us

profile of v6, /device:TPU:1, one launch (start us, length us, event | category | flops | bytes accessed | tf_op | source)
XLA Modules:
  0.0 53.9 jit_solution(5731416311418100777)
XLA Ops:
  0.0 52.4 %tile_attention.1 = bf16[256,128]{1,0:T(8,128)(2,1)} custom-call(s32[64]{0:T(128)} %tile_map_in.1, f32[7,2,7]{2,1,0:T(2,128)} %bitcast.6, bf16[256,128]{1,0:T(8,128)(2,1)} %bitcast.5, f32[1,1024]{1,0:T(1,128)} %bitcast.7, bf16[1024,128]{1,0:T(8,128)(2,1)} %q_weight.1, bf16[1024,128]{1,0:T(8,128)(2,1)} %k_weight.1, bf16[1024,128]{1,0:T(8,128)(2,1)} %v_weight.1, ...), custom_call_target="tpu_custom_call" | custom-call | tf_op jit(solution)/shard_map/tile_attention/pallas_call | solution.py:732
  52.4 1.5 %copy.14 = bf16[1,8,32,128]{3,2,1,0:T(8,128)(2,1)} copy(bf16[1,8,32,128]{3,2,1,0:T(8,128)(2,1)} %bitcast.4) | data formatting | bytes 131072

commit v7 on v5

--- a/solution.py
+++ b/solution.py
@@ -121,9 +121,8 @@
     routed,
     staged,
     halo,
+    attended,
     terms,
-    pair_in,
-    pair_sum,
     line_in,
     load_sem,
     inverse_sem,
@@ -144,8 +143,10 @@
     rim_recv,
     halo_send,
     halo_recv,
-    pair_send,
-    pair_recv,
+    weight_send,
+    weight_recv,
+    attended_send,
+    attended_recv,
     line_send,
     line_recv,
 ):
@@ -207,10 +208,9 @@
         local(v_weight, weights.at[:, 2 * LANES : 3 * LANES], load_sem.at[2]),
         local(q_weight, weights.at[:, 0:LANES], load_sem.at[3]),
         local(picks_in, picks, load_sem.at[4]),
-        local(out_weight, out_w, load_sem.at[5]),
-        local(gain_in, gain, load_sem.at[6]),
-        local(tile_map_in, tile_map, load_sem.at[7]),
-        local(pos_bias_in, pos_bias, load_sem.at[8]),
+        local(gain_in, gain, load_sem.at[5]),
+        local(tile_map_in, tile_map, load_sem.at[6]),
+        local(pos_bias_in, pos_bias, load_sem.at[7]),
     ]
     half_rows = [pl.ds(half * (TOK // 2), TOK // 2) for half in range(2)]
     own_tokens = [
@@ -221,6 +221,13 @@
         load.start()
     for load in loads:
         load.start()
+
+    def out_cols(at, side):
+        return pl.ds(pl.multiple_of((at * CORES + side) * LANES, LANES), LANES)
+
+    for at in range(YL):
+        cols = slice(at * LANES, (at + 1) * LANES)
+        local(out_weight.at[:, out_cols(at, core)], out_w.at[:LANES, cols], load_sem.at[8]).start()
     my_rows = pl.ds(pl.multiple_of(x_at * share, share), share)
     my_cols = pl.ds(pl.multiple_of(my_summ * LANES, LANES), LANES)
     local(sum_keys.at[my_rows, my_cols], keys.at[my_summ], k_recv).start()
@@ -229,7 +236,7 @@
     to_scalars = local(inverse, inverse_s, inverse_sem)
 
     def prepare():
-        loads[7].wait()
+        loads[6].wait()
         lane = lax.broadcasted_iota(jnp.int32, inverse.shape, 1)
 
         def place(at, so_far):
@@ -239,7 +246,7 @@
         to_scalars.start()
 
         loads[0].wait()
-        loads[8].wait()
+        loads[7].wait()
 
         def fill(at, carry):
             rows = pl.ds(pl.multiple_of(at * UNIT, UNIT), UNIT)
@@ -309,6 +316,17 @@
             send_slab(tokens.at[half_rows[half]], my_summ, half, line(step) * CORES + core)
         send_slab(tokens.at[half_rows[half]], my_summ, half, sibling)
 
+    for at in range(YL):
+        cols = slice(at * LANES, (at + 1) * LANES)
+        remote(
+            out_weight.at[:, out_cols(at, 1 - core)],
+            out_w.at[LANES:, cols],
+            weight_send,
+            weight_recv,
+            me,
+            sibling,
+        ).start()
+
     def give(source, held, send_sem, recv_sem, space, summ):
         cols = pl.ds(pl.multiple_of(summ * LANES, LANES), LANES)
         remote(source.at[my_rows, cols], held.at[my_summ], send_sem, recv_sem, space, summ).start()
@@ -382,7 +400,7 @@
         return carry
 
     await_half(0)
-    loads[6].wait()
+    loads[5].wait()
     for load in loads[1:3]:
         load.wait()
     project_half(0)
@@ -585,31 +603,27 @@
             total = total + part_total * factor
             summed = summed + part_sum * factor
         heads.append(summed / total)
-    attended = jnp.concatenate(heads, axis=0).T.astype(jnp.bfloat16)
-
-    loads[5].wait()
-    mixed = jnp.dot(attended, out_w[...], preferred_element_type=jnp.float32).astype(jnp.bfloat16)
+    attended[0] = jnp.concatenate(heads, axis=0).T.astype(jnp.bfloat16)
+
+    share_heads = remote(
+        attended.at[0], attended.at[1], attended_send, attended_recv, me, sibling
+    )
+    share_heads.start()
+    local(out_w.at[:LANES], out_w.at[:LANES], load_sem.at[8]).wait()
+    local(out_w.at[LANES:], out_w.at[LANES:], weight_recv).wait()
+    mixed = jnp.dot(attended[0], out_w[:LANES, :], preferred_element_type=jnp.float32)
+    local(attended.at[1], attended.at[1], attended_recv).wait()
+    mixed = mixed + jnp.dot(attended[1], out_w[LANES:, :], preferred_element_type=jnp.float32)
     for at in range(YL):
-        for side in range(CORES):
-            slab = at * CORES + side
-            terms[side, at] = mixed[:, slab * LANES : (slab + 1) * LANES]
-    order = [line(step) for step in (2, 1, 3, 0)]
-    pair = []
-    for at in order:
-        pair.append(
-            remote(
-                terms.at[1 - core, at], pair_in.at[at], pair_send.at[at], pair_recv.at[at], me, sibling
-            )
-        )
-        pair[-1].start()
+        terms[at] = mixed[:, at * LANES : (at + 1) * LANES].astype(jnp.bfloat16)
     along = []
-    for at in order[:3]:
-        local(pair_in.at[at], pair_in.at[at], pair_recv.at[at]).wait()
-        both = terms[core, at].astype(jnp.float32) + pair_in[at].astype(jnp.float32)
-        pair_sum[at] = both.astype(jnp.bfloat16)
+    rank = jnp.where(y_hi == 0, y_lo, YL - 1 - y_lo)
+    for other in range(YL - 1):
+        other = other + jnp.where(rank <= other, 1, 0)
+        at = jnp.where(y_hi == 0, other, YL - 1 - other)
         along.append(
             remote(
-                pair_sum.at[at],
+                terms.at[at],
                 line_in.at[y_lo],
                 line_send.at[at],
                 line_recv.at[y_lo],
@@ -618,16 +632,16 @@
             )
         )
         along[-1].start()
-    local(pair_in.at[y_lo], pair_in.at[y_lo], pair_recv.at[y_lo]).wait()
-    result = terms[core, y_lo].astype(jnp.float32) + pair_in[y_lo].astype(jnp.float32)
+    result = terms[y_lo].astype(jnp.float32)
     for step in (1, 3, 2):
         at = line(step)
         local(line_in.at[at], line_in.at[at], line_recv.at[at]).wait()
         result = result + line_in[at].astype(jnp.float32)
     out[...] = result.astype(jnp.bfloat16)
 
-    for send in sends + pair + along:
+    for send in sends + [share_heads] + along:
         send.wait_send()
+    local(out_w.at[LANES:], out_w.at[LANES:], weight_send).wait()
     for sem, held in ((k_send, keys), (v_send, values)):
         sent = held.at[: YL * CORES - 1]
         local(sent, sent, sem).wait()
@@ -680,7 +694,7 @@
         pltpu.VMEM((YL * CORES,) + slab, bf16),
         pltpu.VMEM((TOK, D), bf16),
         pltpu.VMEM((D, 3 * LANES), bf16),
-        pltpu.VMEM((LANES, D), bf16),
+        pltpu.VMEM((CORES * LANES, YL * LANES), bf16),
         pltpu.VMEM((TOK + HALO_KEYS, TOK), jnp.int32),
         pltpu.VMEM((SIDE_ROWS, TOK), f32),
         pltpu.VMEM((2, TOK + HALO_KEYS, TOK), f32),
@@ -699,8 +713,7 @@
         pltpu.VMEM((slots, n_space, UNIT, LANES), bf16),
         pltpu.VMEM((slots, n_space, UNIT, LANES), bf16),
         pltpu.VMEM((2 * N_UNIT, UNIT, LANES), bf16),
-        pltpu.VMEM((CORES, YL) + slab, bf16),
-        pltpu.VMEM((YL,) + slab, bf16),
+        pltpu.VMEM((CORES,) + slab, bf16),
         pltpu.VMEM((YL,) + slab, bf16),
         pltpu.VMEM((YL,) + slab, bf16),
         dma((9,)),
@@ -722,8 +735,10 @@
         dma((slots,)),
         dma,
         dma,
-        dma((YL,)),
-        dma((YL,)),
+        dma,
+        dma,
+        dma,
+        dma,
         dma((YL,)),
         dma((YL,)),
     ]

time: 54 us -> 54.2 us (level)
  no operation moved by 1% of the time
where the time goes in v7:
time: 54.2 us; the launch traced here: 54 us
  Pallas kernels  52.5 us (97%)
  local copies, waits for them, and re-layouts  1.47 us (3%)
    pallas_call x1, Pallas kernels, shards(): pl.pallas_call(partial(kernel, n_space), out_shape=jax.ShapeDtypeStruct(s...  52.5 us
    unnamed x1, local copies, waits for them, and re-layouts  1.47 us

profile of v7, /device:TPU:1, one launch (start us, length us, event | category | flops | bytes accessed | tf_op | source)
XLA Modules:
  0.0 54.0 jit_solution(9869268513380835031)
XLA Ops:
  0.0 52.5 %tile_attention.1 = bf16[256,128]{1,0:T(8,128)(2,1)} custom-call(s32[64]{0:T(128)} %tile_map_in.1, f32[7,2,7]{2,1,0:T(2,128)} %bitcast.6, bf16[256,128]{1,0:T(8,128)(2,1)} %bitcast.5, f32[1,1024]{1,0:T(1,128)} %bitcast.7, bf16[1024,128]{1,0:T(8,128)(2,1)} %q_weight.1, bf16[1024,128]{1,0:T(8,128)(2,1)} %k_weight.1, bf16[1024,128]{1,0:T(8,128)(2,1)} %v_weight.1, ...), custom_call_target="tpu_custom_call" | custom-call | tf_op jit(solution)/shard_map/tile_attention/pallas_call | solution.py:745
  52.5 1.5 %copy.14 = bf16[1,8,32,128]{3,2,1,0:T(8,128)(2,1)} copy(bf16[1,8,32,128]{3,2,1,0:T(8,128)(2,1)} %bitcast.4) | data formatting | bytes 131072
